TPU v7x, 512 devices: a whole 4x4x16 slice. The times are simulated.
512 devices in a mesh: ctx: 64 (over x, z), tp: 8 (over y, core).
Axes of the slice: x: 4, y: 4, z: 16, core: 2. Of those that a mesh axis runs over, the one named last changes fastest.
Arguments:
- queries: bfloat16 [65536, 4096], P('ctx', 'tp'), may hold values from -6 to 6
- keys: bfloat16 [65536, 4096], P('ctx', 'tp'), may hold values from -6 to 6
- values: bfloat16 [65536, 4096], P('ctx', 'tp'), may hold values from -23 to 23
- gain: float32 [4096], P('tp'), may hold values from 0.5 to 1.5
Outputs:
- scored: bfloat16 [65536, 4096], P('ctx', 'tp')
All inputs are finite; a program needn't handle non-finite values.
Results may differ from a plain program's by a relative error of at most 0.0049.
Values sent between devices are 32-bit elements; how exact they have to be, the bound alone decides.
No kernel may reach another device: no remote copies, remote signals or barrier semaphores. Data moves between devices by JAX's collectives and lax.ppermute only.
A program may use at most 64 MiB of HBM per device.

v0:
```python
import jax
import jax.numpy as jnp
from jax import lax
from jax.sharding import PartitionSpec as P

HD = 128
D = 4096
BLOCK = 512


def prefix(array, axis, combine, identity):
    count, position = (lax.axis_size(axis), lax.axis_index(axis))
    everything = lax.all_gather(array, axis)
    start = jnp.broadcast_to(jnp.asarray(identity, array.dtype), array.shape)

    def hop(k, before):
        reached = k < position
        new = combine(before, everything[k])
        return jnp.where(reached, new, before)

    return lax.fori_loop(0, count, hop, start)


def add_states(earlier, later):
    return earlier + later


def shards(queries, keys, values, gain):
    tok_rows = queries.shape[0]
    heads_here = queries.shape[1] // HD
    count = tok_rows // BLOCK
    qs = queries.reshape(count, BLOCK, heads_here, HD)
    ks = keys.reshape(count, BLOCK, heads_here, HD)
    vs = values.reshape(count, BLOCK, heads_here, HD)
    block_state = jnp.einsum("bthd,bthe->bhde", ks, vs, preferred_element_type=jnp.float32)
    shard_state = jnp.sum(block_state, axis=0)
    zero_state = jnp.zeros_like(shard_state)
    carried_in = prefix(shard_state, "ctx", add_states, zero_state)
    running = jnp.cumsum(block_state, axis=0) - block_state
    prefix_low = (carried_in[None] + running).astype(jnp.bfloat16)
    carried = jnp.einsum("bthd,bhde->bthe", qs, prefix_low, preferred_element_type=jnp.float32)
    lower = jnp.arange(BLOCK)[:, None] >= jnp.arange(BLOCK)[None, :]
    scores = jnp.einsum("bthd,bshd->bhts", qs, ks, preferred_element_type=jnp.float32)
    scores = jnp.where(lower[None, None], scores, 0.0).astype(jnp.bfloat16)
    local = jnp.einsum("bhts,bshe->bthe", scores, vs, preferred_element_type=jnp.float32)
    mixed = (carried + local).reshape(tok_rows, heads_here * HD)
    partial_sq = jnp.sum(mixed * mixed, axis=1)
    total_sq = lax.psum(partial_sq, "tp")
    meansq = total_sq / D
    scored = mixed / jnp.sqrt(meansq + 1e-06)[:, None] * gain[None, :]
    return scored.astype(jnp.bfloat16)


def solution(mesh):
    return jax.shard_map(
        shards,
        mesh=mesh,
        in_specs=(P("ctx", "tp"), P("ctx", "tp"), P("ctx", "tp"), P("tp")),
        out_specs=P("ctx", "tp"),
        check_vma=False,
    )
```

profile of v0, /device:TPU:1, one launch (start us, length us, event | category | flops | bytes accessed | tf_op | source)
XLA Modules:
  0.0 308.8 jit_solution(7541131765344972132)
XLA Ops:
  6.5 1.3 reshape.29
  8.6 1.3 reshape.28
  9.9 1.2 fusion.18
  11.2 1.3 reshape.30
  12.6 197.2 %all-gather.3.cloned.1.call-done = f32[256,128,128]{2,1,0:T(8,128)} async-done(((f32[4,128,128]{2,1,0:T(8,128)}), f32[256,128,128]{2,1,0:T(8,128)}) %all-gather.3.cloned.1.call-update) | async-done | bytes 16777232 | tf_op jit(solution)/shard_map/all_gather | solution.py:13
  209.8 68.1 %while.14 = (s32[]{:T(128)}, f32[4,128,128]{2,1,0:T(8,128)S(1)}, s32[]{:T(128)}, f32[64,4,128,128]{3,2,1,0:T(8,128)}, s32[]{:T(128)}, /*index=5*/s32[]{:T(128)}) while((s32[]{:T(128)}, f32[4,128,128]{2,1,0:T(8,128)S(1)}, s32[]{:T(128)}, f32[64,4,128,128]{3,2,1,0:T(8,128)}, s32[]{:T(128)}, /*index=5*/s32[]{:T(128)}) %tuple.39), condition=%wide.region_2.3_spmd.clone, body=%wide.region_1.2_spmd.clone.sunk | while | flops 196612 | bytes 786525 | solution.py:21
  210.9 1.0 add_select_fusion.2
  211.9 1.0 add_select_fusion.2
  213.0 1.0 add_select_fusion.2
  214.1 1.0 add_select_fusion.2
  215.1 1.0 add_select_fusion.2
  216.2 1.0 add_select_fusion.2
  217.3 1.0 add_select_fusion.2
  218.3 1.0 add_select_fusion.2
  219.4 1.0 add_select_fusion.2
  220.5 1.0 add_select_fusion.2
  221.5 1.0 add_select_fusion.2
  222.6 1.0 add_select_fusion.2
  223.6 1.0 add_select_fusion.2
  224.7 1.0 add_select_fusion.2
  225.8 1.0 add_select_fusion.2
  226.8 1.0 add_select_fusion.2
  227.9 1.0 add_select_fusion.2
  229.0 1.0 add_select_fusion.2
  230.0 1.0 add_select_fusion.2
  231.1 1.0 add_select_fusion.2
  232.2 1.0 add_select_fusion.2
  233.2 1.0 add_select_fusion.2
  234.3 1.0 add_select_fusion.2
  235.4 1.0 add_select_fusion.2
  236.4 1.0 add_select_fusion.2
  237.5 1.0 add_select_fusion.2
  238.6 1.0 add_select_fusion.2
  239.6 1.0 add_select_fusion.2
  240.7 1.0 add_select_fusion.2
  241.8 1.0 add_select_fusion.2
  242.8 1.0 add_select_fusion.2
  243.9 1.0 add_select_fusion.2
  244.9 1.0 add_select_fusion.2
  246.0 1.0 add_select_fusion.2
  247.1 1.0 add_select_fusion.2
  248.1 1.0 add_select_fusion.2
  249.2 1.0 add_select_fusion.2
  250.3 1.0 add_select_fusion.2
  251.3 1.0 add_select_fusion.2
  252.4 1.0 add_select_fusion.2
  253.5 1.0 add_select_fusion.2
  254.5 1.0 add_select_fusion.2
  255.6 1.0 add_select_fusion.2
  256.7 1.0 add_select_fusion.2
  257.7 1.0 add_select_fusion.2
  258.8 1.0 add_select_fusion.2
  259.9 1.0 add_select_fusion.2
  262.0 1.0 add_select_fusion.2
  263.0 1.0 add_select_fusion.2
  269.4 1.0 add_select_fusion.2
  270.5 1.0 add_select_fusion.2
  275.8 1.0 add_select_fusion.2
  276.9 1.0 add_select_fusion.2
  278.0 1.8 fusion.15
  279.9 5.9 %multiply_reduce_fusion = (f32[2,512]{1,0:T(2,128)S(1)}, f32[2,512,4,128]{1,3,2,0:T(8,128)}) fusion(bf16[2,512,4,128]{1,3,2,0:T(8,128)(2,1)S(1)} %copy.22, pred[512,512]{1,0:T(8,128)(4,1)S(1)} %iota_compare_fusion, bf16[2,512,4,128]{3,2,1,0:T(4,128)(2,1)} %copy-done, bf16[2,512,4,128]{3,2,1,0:T(4,128)(2,1)S(1)} %reshape.30, f32[2,4,128,512]{3,2,1,0:T(8,128)} %fusion.15), kind=kOutput, calls=%fused_computation.10 | convolution fusion | flops 1079507968 | bytes 7606272 | tf_op jit(solution)/shard_map/bhts,bshe->bthe/dot_general | solution.py:45
  285.7 2.0 copy.23
  287.8 12.9 %psum.7 = f32[1024]{0:T(1024)S(1)} all-reduce(f32[1024]{0:T(1024)S(1)} %bitcast.25), channel_id=1, replica_groups=mesh['ctx'=64,'tp'=8] {'tp'}, use_global_device_ids=true, to_apply=%region_5.6 | all-reduce | flops 1024 | bytes 8192 | tf_op jit(solution)/shard_map/psum | solution.py:48
  300.7 1.3 fusion.6
  (23 shorter events, 12.3 us)
Async XLA Ops:
  6.5 203.3 %all-gather.3.cloned.1.call-start = ((), (), s32[]{:S(2)}) async-start(), calls=%async_computation | async-start | bytes 17039360 | tf_op jit(solution)/shard_map/all_gather | solution.py:13
  9.9 1.2 copy-start
  285.7 14.9 %copy-start.1 = (f32[512]{0:T(512)S(1)}, f32[512]{0:T(512)}, u32[]{:S(2)}) copy-start(f32[512]{0:T(512)} %param.9) | copy-start | bytes 6148
Sparse Core Ops, SparseCore 0:
  11.3 198.4 all-gather.2
where the time goes:
time: 311 us; the launch traced here: 309 us
  waiting for transfers between devices  197 us (63%)
  other arithmetic  68 us (22%)
  between operations  13.5 us (4%)
  blocking collectives  12.9 us (4%)
  matrix products  8.91 us (3%)
  local copies, waits for them, and re-layouts  6.75 us (2%)
    all_gather x1, waiting for transfers between devices, prefix(): everything = lax.all_gather(array, axis)  197 us
    select_n x64, other arithmetic, hop(): return jnp.where(reached, new, before)  66.6 us
    psum x1, blocking collectives, shards(): total_sq = lax.psum(partial_sq, 'tp')  12.9 us
  transfers between devices with their start and end apart: 1, of which 1 were waited for; matrix products, arithmetic and copies ran while one was open for 0% of the time, Pallas kernels for 0%

commit v1 on v0

v1 whole, which is shorter than its diff:
```python
import jax
import jax.numpy as jnp
from jax import lax
from jax.sharding import PartitionSpec as P

HD = 128
D = 4096
BLOCK = 512
XS = 4
ZS = 16
NEAR = 4
FAR = ZS // NEAR


def near_groups():
    return [[x * ZS + a * NEAR + b for x in range(XS) for b in range(NEAR)] for a in range(FAR)]


def far_groups():
    return [[x * ZS + a * NEAR + b for a in range(FAR)] for x in range(XS) for b in range(NEAR)]


def exclusive_states(state):
    heads = state.shape[0]
    members = XS * NEAR
    pieces = state.reshape(members, heads * HD // members, HD)
    got = lax.all_to_all(pieces, "ctx", 0, 0, axis_index_groups=near_groups())
    rows = got.reshape(XS, NEAR, *got.shape[1:])
    mine = (lax.axis_index("ctx") % ZS) // NEAR
    group = jnp.sum(rows, axis=1)
    earlier_rows = jnp.cumsum(group, axis=0) - group
    later = (mine < jnp.arange(FAR)).astype(jnp.float32)
    sent = earlier_rows[None] + later[:, None, None, None] * group[None]
    parts = lax.all_to_all(sent, "ctx", 0, 0, axis_index_groups=far_groups())
    start = jnp.sum(parts, axis=0)
    running = [start]
    for b in range(NEAR - 1):
        running.append(running[-1] + rows[:, b])
    back = jnp.stack(running, axis=1).reshape(got.shape)
    mine_back = lax.all_to_all(back, "ctx", 0, 0, axis_index_groups=near_groups())
    return mine_back.reshape(state.shape)


def shards(queries, keys, values, gain):
    tok_rows = queries.shape[0]
    heads_here = queries.shape[1] // HD
    count = tok_rows // BLOCK
    qs = queries.reshape(count, BLOCK, heads_here, HD)
    ks = keys.reshape(count, BLOCK, heads_here, HD)
    vs = values.reshape(count, BLOCK, heads_here, HD)
    block_state = jnp.einsum("bthd,bthe->bhde", ks, vs, preferred_element_type=jnp.float32)
    shard_state = jnp.sum(block_state, axis=0)
    carried_in = exclusive_states(shard_state)
    running = jnp.stack([jnp.zeros_like(block_state[0]), block_state[0]])
    prefix_low = (carried_in[None] + running).astype(jnp.bfloat16)
    carried = jnp.einsum("bthd,bhde->bthe", qs, prefix_low, preferred_element_type=jnp.float32)
    lower = jnp.arange(BLOCK)[:, None] >= jnp.arange(BLOCK)[None, :]
    scores = jnp.einsum("bthd,bshd->bhts", qs, ks, preferred_element_type=jnp.float32)
    scores = jnp.where(lower[None, None], scores, 0.0).astype(jnp.bfloat16)
    local = jnp.einsum("bhts,bshe->bthe", scores, vs, preferred_element_type=jnp.float32)
    mixed = (carried + local).reshape(tok_rows, heads_here * HD)
    partial_sq = jnp.sum(mixed * mixed, axis=1)
    peers = lax.axis_size("tp")
    copies = jnp.broadcast_to(partial_sq[None], (peers, tok_rows))
    total_sq = jnp.sum(lax.all_to_all(copies, "tp", 0, 0), axis=0)
    meansq = total_sq / D
    scored = mixed / jnp.sqrt(meansq + 1e-06)[:, None] * gain[None, :]
    return scored.astype(jnp.bfloat16)


def solution(mesh):
    return jax.shard_map(
        shards,
        mesh=mesh,
        in_specs=(P("ctx", "tp"), P("ctx", "tp"), P("ctx", "tp"), P("tp")),
        out_specs=P("ctx", "tp"),
        check_vma=False,
    )
```

time: 311 us -> 90.1 us (0.29)
  waiting for transfers between devices: 197 us -> 17.5 us
  other arithmetic: 68 us -> 2.37 us
  starting transfers between devices: 0.01 us -> 24.4 us
  blocking collectives: 12.9 us -> 27.7 us
  between operations: 13.5 us -> 0.16 us
    all_gather x1 -> x0, waiting for transfers between devices: 197 us -> none  [prefix(): everything = lax.all_gather(array, axis)]
    select_n x64 -> x0, other arithmetic: 66.6 us -> none  [hop(): return jnp.where(reached, new, before)]
    all_to_all x0 -> x1, blocking collectives: none -> 27.7 us  [exclusive_states(): parts = lax.all_to_all(sent, 'ctx', 0, 0, axis_index_groups=far_groups())]
    all_to_all x0 -> x3, starting transfers between devices: none -> 24.4 us  [the longest x1 9.02 us: exclusive_states(): got = lax.all_to_all(pieces, 'ctx', 0, 0, axis_index_groups=near_groups())]
    all_to_all x0 -> x3, waiting for transfers between devices: none -> 17.5 us  [the longest x1 9.56 us: exclusive_states(): got = lax.all_to_all(pieces, 'ctx', 0, 0, axis_index_groups=near_groups())]
    psum x1 -> x0, blocking collectives: 12.9 us -> none  [shards(): total_sq = lax.psum(partial_sq, 'tp')]
  transfers between devices with their start and end apart: 1 -> 3, of which waited for: 1 -> 3; matrix products, arithmetic and copies ran while one was open for 0% -> 5% of each run, Pallas kernels for 0% -> 0%
where the time goes in v1:
time: 90.1 us; the launch traced here: 89.6 us
  blocking collectives  27.7 us (31%)
  starting transfers between devices  24.4 us (27%)
  waiting for transfers between devices  17.5 us (19%)
  matrix products  9.64 us (11%)
  local copies, waits for them, and re-layouts  7.86 us (9%)
  other arithmetic  2.37 us (3%)
    all_to_all x1, blocking collectives, exclusive_states(): parts = lax.all_to_all(sent, 'ctx', 0, 0, axis_index_groups=far_groups())  27.7 us
    all_to_all x1, waiting for transfers between devices, exclusive_states(): got = lax.all_to_all(pieces, 'ctx', 0, 0, axis_index_groups=near_groups())  9.56 us
    all_to_all x1, starting transfers between devices, exclusive_states(): got = lax.all_to_all(pieces, 'ctx', 0, 0, axis_index_groups=near_groups())  9.02 us
    all_to_all x1, starting transfers between devices, shards(): total_sq = jnp.sum(lax.all_to_all(copies, 'tp', 0, 0), axis=0)  8.06 us
    all_to_all x1, starting transfers between devices, exclusive_states(): lax.all_to_all(back, 'ctx', 0, 0, axis_index_groups=near_groups())  7.31 us
    dot_general x1, matrix products, shards(): jnp.einsum('bhts,bshe->bthe', scores, vs, preferred_element_type=jnp.floa...  5.65 us
    all_to_all x1, waiting for transfers between devices, exclusive_states(): lax.all_to_all(back, 'ctx', 0, 0, axis_index_groups=near_groups())  5.22 us
    dot_general x1, matrix products, shards(): jnp.einsum('bthd,bhde->bthe', qs, prefix_low, preferred_element_type=jnp....  2.79 us
  transfers between devices with their start and end apart: 3, of which 3 were waited for; matrix products, arithmetic and copies ran while one was open for 5% of the time, Pallas kernels for 0%

profile of v1, /device:TPU:1, one launch (start us, length us, event | category | flops | bytes accessed | tf_op | source)
XLA Modules:
  0.0 89.6 jit_solution(9148607400757146967)
XLA Ops:
  0.0 0.0 copy-start
  0.0 1.4 %reshape.69 = bf16[2,512,4,128]{3,2,1,0:T(4,128)(2,1)S(1)} reshape(bf16[1024,512]{1,0:T(8,128)(2,1)} %param.6) | data formatting | bytes 2097152 | tf_op jit(solution)/shard_map/reshape | solution.py:50
  1.4 0.7 copy.46
  2.1 0.0 copy-done
  2.1 0.3 reshape.68
  2.4 1.2 %fusion.23 = (f32[4,128,128]{2,1,0:T(8,128)}, f32[2,4,128,128]{3,2,1,0:T(8,128)S(1)}) fusion(bf16[2,512,4,128]{1,3,2,0:T(8,128)(2,1)S(1)} %copy.46, bf16[2,512,4,128]{3,2,1,0:T(4,128)(2,1)S(1)} %reshape.68), kind=kOutput, calls=%fused_computation.33 | convolution fusion | flops 134283264 | bytes 2883584 | tf_op jit(solution)/shard_map/bthd,bthe->bhde/dot_general | solution.py:51
  3.6 9.0 %all-to-all-start = ((f32[16,32,128]{2,1,0:T(8,128)}), f32[16,32,128]{2,1,0:T(8,128)S(1)}, u32[]{:S(2)}, u32[]{:S(2)}) async-start(f32[16,32,128]{2,1,0:T(8,128)} %bitcast), calls=%async_computation | async-start | bytes 524288 | tf_op jit(solution)/shard_map/all_to_all | solution.py:27
  12.7 9.6 %all-to-all-done = f32[16,32,128]{2,1,0:T(8,128)S(1)} async-done(((f32[16,32,128]{2,1,0:T(8,128)}), f32[16,32,128]{2,1,0:T(8,128)S(1)}, u32[]{:S(2)}, u32[]{:S(2)}) %all-to-all-start) | async-done | bytes 262176 | tf_op jit(solution)/shard_map/all_to_all | solution.py:27
  22.3 0.1 reduce-window_subtract_fusion
  22.4 0.1 multiply_add_fusion
  22.5 27.7 %all_to_all.21 = f32[4,4,32,128]{3,2,1,0:T(8,128)S(1)} all-to-all(f32[4,4,32,128]{3,2,1,0:T(8,128)S(1)} %multiply_add_fusion), channel_id=1, replica_groups={{0,32,64,96},{8,40,72,104},{16,48,80,112},{24,56,88,120},{128,160,192,2..., dimensions={0} | all-to-all | bytes 524288 | tf_op jit(solution)/shard_map/all_to_all | solution.py:34
  50.3 0.7 copy.41
  51.0 7.3 %all-to-all-start.2 = ((f32[16,32,128]{2,1,0:T(8,128)}), f32[16,32,128]{2,1,0:T(8,128)S(1)}, u32[]{:S(2)}, u32[]{:S(2)}) async-start(f32[16,32,128]{2,1,0:T(8,128)} %bitcast.3), calls=%async_computation.2 | async-start | bytes 524288 | tf_op jit(solution)/shard_map/all_to_all | solution.py:40
  58.3 0.7 slice.19
  59.0 1.3 %reshape.73 = bf16[2,512,4,128]{3,2,1,0:T(4,128)(2,1)S(1)} reshape(bf16[1024,512]{1,0:T(8,128)(2,1)} %param.4) | data formatting | bytes 2097152 | tf_op jit(solution)/shard_map/reshape | solution.py:48
  60.4 0.8 iota_compare_fusion
  61.2 5.2 %all-to-all-done.2 = f32[16,32,128]{2,1,0:T(8,128)S(1)} async-done(((f32[16,32,128]{2,1,0:T(8,128)}), f32[16,32,128]{2,1,0:T(8,128)S(1)}, u32[]{:S(2)}, u32[]{:S(2)}) %all-to-all-start.2) | async-done | bytes 262176 | tf_op jit(solution)/shard_map/all_to_all | solution.py:40
  66.4 2.8 %fusion.13 = f32[2,4,128,512]{3,2,1,0:T(8,128)} fusion(bf16[2,512,4,128]{3,2,1,0:T(4,128)(2,1)S(1)} %reshape.73, f32[1,4,128,128]{3,2,1,0:T(8,128)} %slice.19, f32[4,128,128]{2,1,0:T(8,128)S(1)} %bitcast.41), kind=kOutput, calls=%fused_computation.16 | convolution fusion | flops 134479872 | bytes 3670016 | tf_op jit(solution)/shard_map/bthd,bhde->bthe/dot_general | solution.py:56
  69.2 5.7 %multiply_reduce_fusion = (f32[2,512]{1,0:T(2,128)S(1)}, f32[2,512,4,128]{1,3,2,0:T(8,128)}) fusion(bf16[2,512,4,128]{1,3,2,0:T(8,128)(2,1)S(1)} %copy.46, pred[512,512]{1,0:T(8,128)(4,1)} %iota_compare_fusion, bf16[2,512,4,128]{3,2,1,0:T(4,128)(2,1)S(1)} %reshape.68, bf16[2,512,4,128]{3,2,1,0:T(4,128)(2,1)S(1)} %reshape.73, f32[2,4,128,512]{3,2,1,0:T(8,128)} %fusion.13), kind=kOutput, calls=%fused_computation.9 | convolution fusion | flops 1079507968 | bytes 7606272 | tf_op jit(solution)/shard_map/bhts,bshe->bthe/dot_general | solution.py:60
  74.8 0.6 broadcast_in_dim.19
  75.5 8.1 %all-to-all-start.3 = ((f32[8,1,1024]{2,1,0:T(1,128)}), f32[8,1,1024]{2,1,0:T(1,128)S(1)}, u32[]{:S(2)}, u32[]{:S(2)}) async-start(f32[8,1,1024]{2,1,0:T(1,128)} %broadcast_in_dim.19), calls=%async_computation.3 | async-start | bytes 65536 | tf_op jit(solution)/shard_map/all_to_all | solution.py:65
  83.5 0.0 copy-start.1
  83.5 2.0 %copy.47 = f32[2,512,4,128]{3,2,1,0:T(4,128)S(1)} copy(f32[2,512,4,128]{1,3,2,0:T(8,128)} %get-tuple-element.11) | data formatting | bytes 4194304 | tf_op jit(solution)/shard_map/add | solution.py:61
  85.6 2.7 %all-to-all-done.3 = f32[8,1,1024]{2,1,0:T(1,128)S(1)} async-done(((f32[8,1,1024]{2,1,0:T(1,128)}), f32[8,1,1024]{2,1,0:T(1,128)S(1)}, u32[]{:S(2)}, u32[]{:S(2)}) %all-to-all-start.3) | async-done | bytes 32800 | tf_op jit(solution)/shard_map/all_to_all | solution.py:65
  88.3 0.0 copy-done.1
  88.3 1.2 %fusion.6 = bf16[1024,512]{1,0:T(8,128)(2,1)} fusion(f32[128,8,4,128]{3,2,1,0:T(4,128)S(1)} %bitcast.39, f32[512]{0:T(512)S(1)} %copy-done.1, f32[1024]{0:T(1024)S(1)} %add_sqrt_fusion), kind=kLoop, calls=%fused_computation.7 | loop fusion | flops 1572864 | bytes 3151872 | tf_op jit(solution)/shard_map/convert_element_type | solution.py:68
  (8 shorter events, 0.1 us)
Async XLA Ops:
  0.0 2.1 %copy-start = (bf16[1024,512]{1,0:T(8,128)(2,1)S(1)}, bf16[1024,512]{1,0:T(8,128)(2,1)}, u32[]{:S(2)}) copy-start(bf16[1024,512]{1,0:T(8,128)(2,1)} %param.5) | copy-start | bytes 3145732
  3.6 18.6 %all-to-all-start = ((f32[16,32,128]{2,1,0:T(8,128)}), f32[16,32,128]{2,1,0:T(8,128)S(1)}, u32[]{:S(2)}, u32[]{:S(2)}) async-start(f32[16,32,128]{2,1,0:T(8,128)} %bitcast), calls=%async_computation | async-start | bytes 524288 | tf_op jit(solution)/shard_map/all_to_all | solution.py:27
  51.0 15.4 %all-to-all-start.2 = ((f32[16,32,128]{2,1,0:T(8,128)}), f32[16,32,128]{2,1,0:T(8,128)S(1)}, u32[]{:S(2)}, u32[]{:S(2)}) async-start(f32[16,32,128]{2,1,0:T(8,128)} %bitcast.3), calls=%async_computation.2 | async-start | bytes 524288 | tf_op jit(solution)/shard_map/all_to_all | solution.py:40
  75.5 12.8 %all-to-all-start.3 = ((f32[8,1,1024]{2,1,0:T(1,128)}), f32[8,1,1024]{2,1,0:T(1,128)S(1)}, u32[]{:S(2)}, u32[]{:S(2)}) async-start(f32[8,1,1024]{2,1,0:T(1,128)} %broadcast_in_dim.19), calls=%async_computation.3 | async-start | bytes 65536 | tf_op jit(solution)/shard_map/all_to_all | solution.py:65
  83.5 4.8 %copy-start.1 = (f32[512]{0:T(512)S(1)}, f32[512]{0:T(512)}, u32[]{:S(2)}) copy-start(f32[512]{0:T(512)} %param.7) | copy-start | bytes 6148

commit v2 on v1

v2 whole, which is shorter than its diff:
```python
import jax
import jax.numpy as jnp
from jax import lax
from jax.experimental import pallas as pl
from jax.experimental.pallas import tpu as pltpu
from jax.sharding import PartitionSpec as P

HD = 128
D = 4096
BLOCK = 512
XS = 4
ZS = 16
NEAR = 4
FAR = ZS // NEAR
MEMBERS = XS * NEAR
PEERS = 8
LOAD = 128
CHUNK = 256
STORE = 128
VMEM = pl.BlockSpec(memory_space=pltpu.VMEM)
HBM = pl.BlockSpec(memory_space=pltpu.HBM)
STATE_MIB = 53.2
MIXED_MIB = 32
OTHER_MIB = 32


def grant(mib):
    return pltpu.CompilerParams(vmem_limit_bytes=int(mib * 1024 * 1024))


def near_groups():
    return [[x * ZS + a * NEAR + b for x in range(XS) for b in range(NEAR)] for a in range(FAR)]


def far_groups():
    return [[x * ZS + a * NEAR + b for a in range(FAR)] for x in range(XS) for b in range(NEAR)]


def contract_tokens(left, right):
    return lax.dot_general(left, right, (((0,), (0,)), ((), ())), preferred_element_type=jnp.float32)


def contract_last(left, right):
    return lax.dot_general(left, right, (((1,), (1,)), ((), ())), preferred_element_type=jnp.float32)


def head_columns(h):
    return slice(h * HD, (h + 1) * HD)


def state_kernel(keys, values, total, key_rows, value_rows, sems):
    rows, width = keys.shape
    parts = rows // LOAD
    copies = []
    for c in range(parts):
        at = pl.ds(c * LOAD, LOAD)
        pair = (
            pltpu.make_async_copy(keys.at[at], key_rows.at[at], sems.at[c]),
            pltpu.make_async_copy(values.at[at], value_rows.at[at], sems.at[parts + c]),
        )
        for copy in pair:
            copy.start()
        copies.append(pair)
    sums = [None] * (width // HD)
    for c in range(0, rows, CHUNK):
        for pair in copies[c // LOAD : (c + CHUNK) // LOAD]:
            for copy in pair:
                copy.wait()
        for h in range(len(sums)):
            cols = head_columns(h)
            part = contract_tokens(key_rows[c : c + CHUNK, cols], value_rows[c : c + CHUNK, cols])
            sums[h] = part if c == 0 else sums[h] + part
    for h, s in enumerate(sums):
        total[h] = s


def shard_state(keys, values):
    rows, width = keys.shape
    return pl.pallas_call(
        state_kernel,
        in_specs=[HBM, HBM],
        out_specs=VMEM,
        out_shape=jax.ShapeDtypeStruct((width // HD, HD, HD), jnp.float32),
        scratch_shapes=[
            pltpu.VMEM((rows, width), keys.dtype),
            pltpu.VMEM((rows, width), values.dtype),
            pltpu.SemaphoreType.DMA((2 * rows // LOAD,)),
        ],
        compiler_params=grant(STATE_MIB),
        cost_estimate=pl.CostEstimate(flops=2 * rows * width * HD, bytes_accessed=4 * rows * width, transcendentals=0),
        name="states",
    )(keys, values)


def sent_kernel(got, sent):
    mine = (lax.axis_index("ctx") // NEAR) % FAR
    group, earlier = [], []
    for x in range(XS):
        g = got[x * NEAR]
        for b in range(1, NEAR):
            g = g + got[x * NEAR + b]
        group.append(g)
    e = jnp.zeros_like(group[0])
    for x in range(XS):
        earlier.append(e)
        e = e + group[x]
    for a in range(FAR):
        later = jnp.where(mine < a, 1.0, 0.0).astype(jnp.float32)
        for x in range(XS):
            sent[a, x] = earlier[x] + later * group[x]


def back_kernel(parts, got, back):
    for x in range(XS):
        run = parts[0, x]
        for a in range(1, FAR):
            run = run + parts[a, x]
        for b in range(NEAR):
            back[x * NEAR + b] = run
            if b < NEAR - 1:
                run = run + got[x * NEAR + b]


def exclusive_states(state):
    rows = state.shape[0] * HD // MEMBERS
    pieces = state.reshape(MEMBERS, rows, HD)
    got = lax.all_to_all(pieces, "ctx", 0, 0, axis_index_groups=near_groups())
    sent = pl.pallas_call(
        sent_kernel,
        in_specs=[VMEM],
        out_specs=VMEM,
        out_shape=jax.ShapeDtypeStruct((FAR, XS, rows, HD), jnp.float32),
        compiler_params=grant(OTHER_MIB),
        name="sent",
    )(got)
    parts = lax.all_to_all(sent, "ctx", 0, 0, axis_index_groups=far_groups())
    back = pl.pallas_call(
        back_kernel,
        in_specs=[VMEM, VMEM],
        out_specs=VMEM,
        out_shape=jax.ShapeDtypeStruct(got.shape, jnp.float32),
        compiler_params=grant(OTHER_MIB),
        name="back",
    )(parts, got)
    mine = lax.all_to_all(back, "ctx", 0, 0, axis_index_groups=near_groups())
    return mine.reshape(state.shape)


def mixed_kernel(queries, keys, values, prefix, mixed, squares):
    half = BLOCK // 2
    tiles = BLOCK // HD
    row = lax.broadcasted_iota(jnp.int32, (half, half), 0)
    col = lax.broadcasted_iota(jnp.int32, (half, half), 1)
    lower = row >= col
    for start in range(0, queries.shape[0], BLOCK):
        top_rows = slice(start, start + half)
        low_rows = slice(start + half, start + BLOCK)
        acc = [None, None]
        for h in range(queries.shape[1] // HD):
            cols = head_columns(h)
            state = prefix[h]
            if start:
                state = state + contract_tokens(keys[:start, cols], values[:start, cols])
            state = state.astype(jnp.bfloat16)
            q, k = queries[top_rows, cols], keys[top_rows, cols]
            top = jnp.where(lower, contract_last(q, k), 0.0).astype(jnp.bfloat16)
            m = jnp.dot(q, state, preferred_element_type=jnp.float32)
            m = m + jnp.dot(top, values[top_rows, cols], preferred_element_type=jnp.float32)
            mixed[top_rows, cols] = m
            acc[0] = m * m if h == 0 else acc[0] + m * m
            q = queries[low_rows, cols]
            side = contract_last(q, k).astype(jnp.bfloat16)
            low = jnp.where(lower, contract_last(q, keys[low_rows, cols]), 0.0).astype(jnp.bfloat16)
            both = jnp.concatenate([side, low], axis=1)
            m = jnp.dot(q, state, preferred_element_type=jnp.float32)
            m = m + jnp.dot(both, values[start : start + BLOCK, cols], preferred_element_type=jnp.float32)
            mixed[low_rows, cols] = m
            acc[1] = m * m if h == 0 else acc[1] + m * m
        for i, a in enumerate(acc):
            turned = jnp.swapaxes(a.reshape(tiles // 2, HD, HD), 1, 2)
            sums = jnp.sum(turned, axis=1)
            at = start // HD + i * (tiles // 2)
            for p in range(PEERS):
                squares[p, at : at + tiles // 2] = sums


def mixed_part(queries, keys, values, prefix):
    rows, width = queries.shape
    return pl.pallas_call(
        mixed_kernel,
        in_specs=[VMEM] * 4,
        out_specs=[VMEM] * 2,
        out_shape=[
            jax.ShapeDtypeStruct((rows, width), jnp.float32),
            jax.ShapeDtypeStruct((PEERS, rows // HD, HD), jnp.float32),
        ],
        compiler_params=grant(MIXED_MIB),
        cost_estimate=pl.CostEstimate(flops=4 * rows * BLOCK * width, bytes_accessed=10 * rows * width, transcendentals=0),
        name="mixed",
    )(queries, keys, values, prefix)


def scored_kernel(mixed, squares, gain, out, rows, sems):
    total = squares[0]
    for p in range(1, PEERS):
        total = total + squares[p]
    scale = lax.rsqrt(total / D + 1e-06)
    copies = []
    for t in range(mixed.shape[0] // HD):
        at = slice(t * HD, (t + 1) * HD)
        column = jnp.swapaxes(jnp.broadcast_to(scale[t : t + 1], (HD, HD)), 0, 1)
        for h in range(mixed.shape[1] // HD):
            cols = head_columns(h)
            rows[at, cols] = (mixed[at, cols] * column * gain[:, cols]).astype(jnp.bfloat16)
        part = pl.ds(t * HD, HD)
        copies.append(pltpu.make_async_copy(rows.at[part], out.at[part], sems.at[t]))
        copies[-1].start()
    for copy in copies:
        copy.wait()


def scored_part(mixed, squares, gain):
    rows, width = mixed.shape
    return pl.pallas_call(
        scored_kernel,
        in_specs=[VMEM] * 3,
        out_specs=HBM,
        out_shape=jax.ShapeDtypeStruct((rows, width), jnp.bfloat16),
        scratch_shapes=[pltpu.VMEM((rows, width), jnp.bfloat16), pltpu.SemaphoreType.DMA((rows // HD,))],
        compiler_params=grant(OTHER_MIB),
        name="scored",
    )(mixed, squares, gain.reshape(1, width))


def shards(queries, keys, values, gain):
    total = shard_state(keys, values)
    prefix = exclusive_states(total)
    mixed, squares = mixed_part(queries, keys, values, prefix)
    squares = lax.all_to_all(squares, "tp", 0, 0)
    return scored_part(mixed, squares, gain)


def solution(mesh):
    return jax.shard_map(
        shards,
        mesh=mesh,
        in_specs=(P("ctx", "tp"), P("ctx", "tp"), P("ctx", "tp"), P("tp")),
        out_specs=P("ctx", "tp"),
        check_vma=False,
    )
```

time: 90.1 us -> 81.2 us (0.901)
  blocking collectives: 27.7 us -> 73.9 us
  starting transfers between devices: 24.4 us -> 0 us
  waiting for transfers between devices: 17.5 us -> 0 us
  matrix products: 9.64 us -> 0 us
  local copies, waits for them, and re-layouts: 7.86 us -> 0.01 us
  Pallas kernels: 0 us -> 7.07 us
  other arithmetic: 2.37 us -> 0 us
    all_to_all x0 -> x3, blocking collectives: none -> 46.3 us  [the longest x1 18.5 us: exclusive_states(): got = lax.all_to_all(pieces, 'ctx', 0, 0, axis_index_groups=near_groups())]
    all_to_all x3 -> x0, starting transfers between devices: 24.4 us -> none  [the longest x1 9.02 us: exclusive_states(): got = lax.all_to_all(pieces, 'ctx', 0, 0, axis_index_groups=near_groups())]
    all_to_all x3 -> x0, waiting for transfers between devices: 17.5 us -> none  [the longest x1 9.56 us: exclusive_states(): got = lax.all_to_all(pieces, 'ctx', 0, 0, axis_index_groups=near_groups())]
    dot_general x3 -> x0, matrix products: 9.64 us -> none  [the longest x1 5.65 us: shards(): jnp.einsum('bhts,bshe->bthe', scores, vs, preferred_element_type=jnp.floa...]
    pallas_call x0 -> x5, Pallas kernels: none -> 7.07 us  [the longest x1 3.37 us: mixed_part(): pl.pallas_call(mixed_kernel, in_specs=[VMEM] * 4, out_specs=[VMEM] * 2, o...]
    reshape x4 -> x0, local copies, waits for them, and re-layouts: 3.72 us -> none  [the longest x2 2.1 us: shards(): vs = values.reshape(count, BLOCK, heads_here, HD)]
    add x1 -> x0, local copies, waits for them, and re-layouts: 2.03 us -> none  [shards(): mixed = (carried + local).reshape(tok_rows, heads_here * HD)]
    convert_element_type x2 -> x0, other arithmetic: 1.25 us -> none  [the longest x1 1.25 us: shards(): return scored.astype(jnp.bfloat16)]
  transfers between devices with their start and end apart: 3 -> 0, of which waited for: 3 -> 0; matrix products, arithmetic and copies ran while one was open for 5% -> 0% of each run, Pallas kernels for 0% -> 0%
where the time goes in v2:
time: 81.2 us; the launch traced here: 81 us
  blocking collectives  73.9 us (91%)
  Pallas kernels  7.07 us (9%)
    all_to_all x1, blocking collectives, exclusive_states(): parts = lax.all_to_all(sent, 'ctx', 0, 0, axis_index_groups=far_groups())  27.6 us
    all_to_all x1, blocking collectives, exclusive_states(): got = lax.all_to_all(pieces, 'ctx', 0, 0, axis_index_groups=near_groups())  18.5 us
    all_to_all x1, blocking collectives, exclusive_states(): mine = lax.all_to_all(back, 'ctx', 0, 0, axis_index_groups=near_groups())  15.2 us
    all_to_all x1, blocking collectives, shards(): squares = lax.all_to_all(squares, 'tp', 0, 0)  12.6 us
    pallas_call x1, Pallas kernels, mixed_part(): pl.pallas_call(mixed_kernel, in_specs=[VMEM] * 4, out_specs=[VMEM] * 2, o...  3.37 us
    pallas_call x1, Pallas kernels, shard_state(): pl.pallas_call(state_kernel, in_specs=[HBM, HBM], out_specs=VMEM, out_sha...  2.47 us

profile of v2, /device:TPU:1, one launch (start us, length us, event | category | flops | bytes accessed | tf_op | source)
XLA Modules:
  0.0 81.0 jit_solution(15826728149807395268)
XLA Ops:
  0.0 0.0 copy-start.1
  0.0 0.0 copy-start
  0.0 0.0 copy-start.3
  0.0 2.5 %states.1 = f32[4,128,128]{2,1,0:T(8,128)S(1)} custom-call(bf16[1024,512]{1,0:T(8,128)(2,1)} %keys.3, bf16[1024,512]{1,0:T(8,128)(2,1)} %values.3), custom_call_target="tpu_custom_call" | custom-call | flops 134217728 | bytes 2097152 | tf_op jit(solution)/shard_map/states/pallas_call | solution.py:79
  2.5 18.5 %all_to_all.20.got = f32[16,32,128]{2,1,0:T(8,128)S(1)} all-to-all(f32[16,32,128]{2,1,0:T(8,128)S(1)} %bitcast.3), channel_id=1, replica_groups={{0,8,16,24,128,136,144,152,256,264,272,280,384,392,400,408},{32,40,48,5..., dimensions={0} | all-to-all | bytes 524288 | tf_op jit(solution)/shard_map/all_to_all | solution.py:127
  21.0 27.6 %all_to_all.21.parts = f32[4,4,32,128]{3,2,1,0:T(8,128)S(1)} all-to-all(f32[4,4,32,128]{3,2,1,0:T(8,128)S(1)} %sent.1), channel_id=1, replica_groups={{0,32,64,96},{8,40,72,104},{16,48,80,112},{24,56,88,120},{128,160,192,2..., dimensions={0} | all-to-all | bytes 524288 | tf_op jit(solution)/shard_map/all_to_all | solution.py:136
  48.7 15.2 %all_to_all.22 = f32[16,32,128]{2,1,0:T(8,128)S(1)} all-to-all(f32[16,32,128]{2,1,0:T(8,128)S(1)} %back.1), channel_id=1, replica_groups={{0,8,16,24,128,136,144,152,256,264,272,280,384,392,400,408},{32,40,48,5..., dimensions={0} | all-to-all | bytes 524288 | tf_op jit(solution)/shard_map/all_to_all | solution.py:145
  63.9 0.0 copy-start.2
  63.9 0.0 copy-done.1
  63.9 0.0 copy-done
  63.9 0.0 copy-done.3
  63.9 3.4 %mixed.1 = (f32[1024,512]{1,0:T(8,128)S(1)}, f32[8,8,128]{2,1,0:T(8,128)S(1)}) custom-call(bf16[1024,512]{1,0:T(8,128)(2,1)S(1)} %copy-done.3, bf16[1024,512]{1,0:T(8,128)(2,1)S(1)} %copy-done, bf16[1024,512]{1,0:T(8,128)(2,1)S(1)} %copy-done.1, f32[4,128,128]{2,1,0:T(8,128)S(1)} %bitcast.4), custom_call_target="tpu_custom_call" | custom-call | flops 1073741824 | bytes 5242880 | tf_op jit(solution)/shard_map/mixed/pallas_call | solution.py:189
  67.3 12.6 %all_to_all.23.squares = f32[8,8,128]{2,1,0:T(8,128)S(1)} all-to-all(f32[8,8,128]{2,1,0:T(8,128)S(1)} %get-tuple-element.8), channel_id=1, replica_groups=mesh['ctx'=64,'tp'=8] {'tp'}, dimensions={0} | all-to-all | bytes 65536 | tf_op jit(solution)/shard_map/all_to_all | solution.py:239
  79.8 0.0 copy-done.2
  79.8 1.2 %scored.1 = bf16[1024,512]{1,0:T(8,128)(2,1)} custom-call(f32[1024,512]{1,0:T(8,128)S(1)} %get-tuple-element.7.mixed, f32[8,8,128]{2,1,0:T(8,128)S(1)} %all_to_all.23.squares, f32[1,512]{1,0:T(1,128)S(1)} %bitcast.5), custom_call_target="tpu_custom_call" | custom-call | tf_op jit(solution)/shard_map/scored/pallas_call | solution.py:224
  (2 shorter events, 0.1 us)
Async XLA Ops:
  0.0 63.9 %copy-start.1 = (bf16[1024,512]{1,0:T(8,128)(2,1)S(1)}, bf16[1024,512]{1,0:T(8,128)(2,1)}, u32[]{:S(2)}) copy-start(bf16[1024,512]{1,0:T(8,128)(2,1)} %values.3) | copy-start | bytes 3145732
  0.0 63.9 %copy-start = (bf16[1024,512]{1,0:T(8,128)(2,1)S(1)}, bf16[1024,512]{1,0:T(8,128)(2,1)}, u32[]{:S(2)}) copy-start(bf16[1024,512]{1,0:T(8,128)(2,1)} %keys.3) | copy-start | bytes 3145732
  0.0 63.9 %copy-start.3 = (bf16[1024,512]{1,0:T(8,128)(2,1)S(1)}, bf16[1024,512]{1,0:T(8,128)(2,1)}, u32[]{:S(2)}) copy-start(bf16[1024,512]{1,0:T(8,128)(2,1)} %queries.1) | copy-start | bytes 3145732
  63.9 16.0 %copy-start.2 = (f32[512]{0:T(512)S(1)}, f32[512]{0:T(512)}, u32[]{:S(2)}) copy-start(f32[512]{0:T(512)} %param.7) | copy-start | bytes 6148

commit v3 on v2

--- a/solution.py
+++ b/solution.py
@@ -32,8 +32,8 @@
     return [[x * ZS + a * NEAR + b for x in range(XS) for b in range(NEAR)] for a in range(FAR)]
 
 
-def far_groups():
-    return [[x * ZS + a * NEAR + b for a in range(FAR)] for x in range(XS) for b in range(NEAR)]
+def between(pairs):
+    return [(x * ZS + i * NEAR + b, x * ZS + j * NEAR + b) for x in range(XS) for b in range(NEAR) for i, j in pairs]
 
 
 def contract_tokens(left, right):
@@ -92,33 +92,51 @@
     )(keys, values)
 
 
-def sent_kernel(got, sent):
+STEPS = (
+    ((2, 0),),
+    ((3, 0),),
+    ((1, 0), (0, 1)),
+    ((0, 3),),
+    ((0, 2), (2, 1)),
+    ((1, 3), (3, 1)),
+    ((1, 2),),
+    ((2, 3), (3, 2)),
+)
+
+
+def own_kernel(got, *outs):
+    run = None
+    for x in range(XS):
+        for b in range(NEAR):
+            run = got[x * NEAR + b] if run is None else run + got[x * NEAR + b]
+        for out in outs:
+            out[x] = run
+
+
+def back_kernel(got, *rest):
+    parts, back = rest[:-1], rest[-1]
     mine = (lax.axis_index("ctx") // NEAR) % FAR
-    group, earlier = [], []
+    run = None
     for x in range(XS):
-        g = got[x * NEAR]
-        for b in range(1, NEAR):
-            g = g + got[x * NEAR + b]
-        group.append(g)
-    e = jnp.zeros_like(group[0])
-    for x in range(XS):
-        earlier.append(e)
-        e = e + group[x]
-    for a in range(FAR):
-        later = jnp.where(mine < a, 1.0, 0.0).astype(jnp.float32)
-        for x in range(XS):
-            sent[a, x] = earlier[x] + later * group[x]
-
-
-def back_kernel(parts, got, back):
-    for x in range(XS):
-        run = parts[0, x]
-        for a in range(1, FAR):
-            run = run + parts[a, x]
+        start = jnp.zeros(got.shape[1:], jnp.float32) if run is None else run
+        run = start
+        for step, part in zip(STEPS, parts):
+            shifted = [dst for src, dst in step if src > dst]
+            if not shifted:
+                start = start + part[x]
+            elif len(shifted) == len(step):
+                start = start + part[x - 1] if x else start
+            else:
+                moved = mine == shifted[0]
+                for dst in shifted[1:]:
+                    moved = moved | (mine == dst)
+                before = part[x - 1] if x else jnp.zeros_like(start)
+                start = start + jnp.where(moved, before, part[x])
         for b in range(NEAR):
-            back[x * NEAR + b] = run
+            back[x * NEAR + b] = start
             if b < NEAR - 1:
-                run = run + got[x * NEAR + b]
+                start = start + got[x * NEAR + b]
+            run = run + got[x * NEAR + b]
 
 
 def exclusive_states(state):
@@ -126,22 +144,22 @@
     pieces = state.reshape(MEMBERS, rows, HD)
     got = lax.all_to_all(pieces, "ctx", 0, 0, axis_index_groups=near_groups())
     sent = pl.pallas_call(
-        sent_kernel,
+        own_kernel,
         in_specs=[VMEM],
-        out_specs=VMEM,
-        out_shape=jax.ShapeDtypeStruct((FAR, XS, rows, HD), jnp.float32),
+        out_specs=[VMEM] * len(STEPS),
+        out_shape=[jax.ShapeDtypeStruct((XS, rows, HD), jnp.float32)] * len(STEPS),
         compiler_params=grant(OTHER_MIB),
         name="sent",
     )(got)
-    parts = lax.all_to_all(sent, "ctx", 0, 0, axis_index_groups=far_groups())
+    parts = [lax.ppermute(out, "ctx", between(step)) for out, step in zip(sent, STEPS)]
     back = pl.pallas_call(
         back_kernel,
-        in_specs=[VMEM, VMEM],
+        in_specs=[VMEM] * (1 + len(parts)),
         out_specs=VMEM,
         out_shape=jax.ShapeDtypeStruct(got.shape, jnp.float32),
         compiler_params=grant(OTHER_MIB),
         name="back",
-    )(parts, got)
+    )(got, *parts)
     mine = lax.all_to_all(back, "ctx", 0, 0, axis_index_groups=near_groups())
     return mine.reshape(state.shape)
 

time: 81.2 us -> 74.2 us (0.914)
  the two profiles are of different devices: /device:TPU:1 before, /device:TPU:384 now
where the time goes in v3:
time: 74.2 us; the launch traced here: 73.9 us
  blocking collectives  43.4 us (58%)
  starting transfers between devices  14.7 us (20%)
  waiting for transfers between devices  8.56 us (12%)
  Pallas kernels  7.1 us (10%)
    all_to_all x1, blocking collectives, exclusive_states(): mine = lax.all_to_all(back, 'ctx', 0, 0, axis_index_groups=near_groups())  17.3 us
    all_to_all x1, blocking collectives, exclusive_states(): got = lax.all_to_all(pieces, 'ctx', 0, 0, axis_index_groups=near_groups())  16.5 us
    ppermute x8, starting transfers between devices, exclusive_states(): lax.ppermute(out, 'ctx', between(step))  14.7 us
    all_to_all x1, blocking collectives, shards(): squares = lax.all_to_all(squares, 'tp', 0, 0)  9.69 us
    ppermute x8, waiting for transfers between devices, exclusive_states(): lax.ppermute(out, 'ctx', between(step))  8.56 us
    pallas_call x1, Pallas kernels, mixed_part(): pl.pallas_call(mixed_kernel, in_specs=[VMEM] * 4, out_specs=[VMEM] * 2, o...  3.37 us
    pallas_call x1, Pallas kernels, shard_state(): pl.pallas_call(state_kernel, in_specs=[HBM, HBM], out_specs=VMEM, out_sha...  2.47 us
  transfers between devices with their start and end apart: 8, of which 2 were waited for; matrix products, arithmetic and copies ran while one was open for 0% of the time, Pallas kernels for 0%

profile of v3, /device:TPU:384, one launch (start us, length us, event | category | flops | bytes accessed | tf_op | source)
XLA Modules:
  0.0 73.9 jit_solution(17928961683801932540)
XLA Ops:
  0.0 0.0 copy-start.1
  0.0 0.0 copy-start
  0.0 0.0 copy-start.3
  0.0 2.5 %states.1 = f32[4,128,128]{2,1,0:T(8,128)S(1)} custom-call(bf16[1024,512]{1,0:T(8,128)(2,1)} %keys.3, bf16[1024,512]{1,0:T(8,128)(2,1)} %values.3), custom_call_target="tpu_custom_call" | custom-call | flops 134217728 | bytes 2097152 | tf_op jit(solution)/shard_map/states/pallas_call | solution.py:79
  2.5 16.5 %all_to_all.15.got = f32[16,32,128]{2,1,0:T(8,128)S(1)} all-to-all(f32[16,32,128]{2,1,0:T(8,128)S(1)} %bitcast.3), channel_id=1, replica_groups={{0,8,16,24,128,136,144,152,256,264,272,280,384,392,400,408},{32,40,48,5..., dimensions={0} | all-to-all | bytes 524288 | tf_op jit(solution)/shard_map/all_to_all | solution.py:145
  19.0 0.7 collective-permute-start
  19.7 1.3 %collective-permute-start.1 = (f32[4,32,128]{2,1,0:T(8,128)S(1)}, f32[4,32,128]{2,1,0:T(8,128)S(1)}, u32[]{:S(2)}, u32[]{:S(2)}) collective-permute-start(f32[4,32,128]{2,1,0:T(8,128)S(1)} %get-tuple-element.16), channel_id=1, source_target_pairs={{96,0},{104,8},{112,16},{120,24},{224,128},{232,136},{240,144},{24... | collective-permute-start | bytes 196616 | tf_op jit(solution)/shard_map/ppermute | solution.py:154
  21.0 0.7 collective-permute-start.2
  21.6 1.3 %collective-permute-start.3 = (f32[4,32,128]{2,1,0:T(8,128)S(1)}, f32[4,32,128]{2,1,0:T(8,128)S(1)}, u32[]{:S(2)}, u32[]{:S(2)}) collective-permute-start(f32[4,32,128]{2,1,0:T(8,128)S(1)} %get-tuple-element.18), channel_id=1, source_target_pairs={{0,96},{8,104},{16,112},{24,120},{128,224},{136,232},{144,240},{15... | collective-permute-start | bytes 196616 | tf_op jit(solution)/shard_map/ppermute | solution.py:154
  22.9 0.7 collective-permute-start.4
  23.6 0.0 collective-permute-done.rest_0_
  23.6 7.0 %collective-permute-start.5 = (f32[4,32,128]{2,1,0:T(8,128)S(1)}, f32[4,32,128]{2,1,0:T(8,128)S(1)}, u32[]{:S(2)}, u32[]{:S(2)}) collective-permute-start(f32[4,32,128]{2,1,0:T(8,128)S(1)} %get-tuple-element.20), channel_id=1, source_target_pairs={{32,96},{96,32},{40,104},{104,40},{48,112},{112,48},{56,120},{120,... | collective-permute-start | bytes 196616 | tf_op jit(solution)/shard_map/ppermute | solution.py:154
  30.6 0.0 collective-permute-done.1.rest_1_
  30.6 0.7 collective-permute-start.6
  31.3 0.0 collective-permute-done.2.rest_2_
  31.3 2.5 %collective-permute-start.7 = (f32[4,32,128]{2,1,0:T(8,128)S(1)}, f32[4,32,128]{2,1,0:T(8,128)S(1)}, u32[]{:S(2)}, u32[]{:S(2)}) collective-permute-start(f32[4,32,128]{2,1,0:T(8,128)S(1)} %get-tuple-element.22), channel_id=1, source_target_pairs={{64,96},{96,64},{72,104},{104,72},{80,112},{112,80},{88,120},{120,... | collective-permute-start | bytes 196616 | tf_op jit(solution)/shard_map/ppermute | solution.py:154
  33.8 0.0 collective-permute-done.3.rest_3_
  33.8 0.0 collective-permute-done.4.rest_4_
  33.8 6.9 %collective-permute-done.5.rest_5_ = f32[4,32,128]{2,1,0:T(8,128)S(1)} collective-permute-done((f32[4,32,128]{2,1,0:T(8,128)S(1)}, f32[4,32,128]{2,1,0:T(8,128)S(1)}, u32[]{:S(2)}, u32[]{:S(2)}) %collective-permute-start.5) | collective-permute-done | bytes 65568 | tf_op jit(solution)/shard_map/ppermute | solution.py:154
  40.6 0.0 collective-permute-done.6.rest_6_
  40.6 1.7 %collective-permute-done.7.rest_7_ = f32[4,32,128]{2,1,0:T(8,128)S(1)} collective-permute-done((f32[4,32,128]{2,1,0:T(8,128)S(1)}, f32[4,32,128]{2,1,0:T(8,128)S(1)}, u32[]{:S(2)}, u32[]{:S(2)}) %collective-permute-start.7) | collective-permute-done | bytes 65568 | tf_op jit(solution)/shard_map/ppermute | solution.py:154
  42.3 0.1 back.1
  42.4 17.3 %all_to_all.16 = f32[16,32,128]{2,1,0:T(8,128)S(1)} all-to-all(f32[16,32,128]{2,1,0:T(8,128)S(1)} %back.1), channel_id=1, replica_groups={{0,8,16,24,128,136,144,152,256,264,272,280,384,392,400,408},{32,40,48,5..., dimensions={0} | all-to-all | bytes 524288 | tf_op jit(solution)/shard_map/all_to_all | solution.py:163
  59.7 0.0 copy-start.2
  59.7 0.0 copy-done.1
  59.7 0.0 copy-done
  59.7 0.0 copy-done.3
  59.7 3.4 %mixed.1 = (f32[1024,512]{1,0:T(8,128)S(1)}, f32[8,8,128]{2,1,0:T(8,128)S(1)}) custom-call(bf16[1024,512]{1,0:T(8,128)(2,1)S(1)} %copy-done.3, bf16[1024,512]{1,0:T(8,128)(2,1)S(1)} %copy-done, bf16[1024,512]{1,0:T(8,128)(2,1)S(1)} %copy-done.1, f32[4,128,128]{2,1,0:T(8,128)S(1)} %bitcast.4), custom_call_target="tpu_custom_call" | custom-call | flops 1073741824 | bytes 5242880 | tf_op jit(solution)/shard_map/mixed/pallas_call | solution.py:207
  63.1 9.7 %all_to_all.17.squares = f32[8,8,128]{2,1,0:T(8,128)S(1)} all-to-all(f32[8,8,128]{2,1,0:T(8,128)S(1)} %get-tuple-element.24), channel_id=1, replica_groups=mesh['ctx'=64,'tp'=8] {'tp'}, dimensions={0} | all-to-all | bytes 65536 | tf_op jit(solution)/shard_map/all_to_all | solution.py:257
  72.7 0.0 copy-done.2
  72.7 1.2 %scored.1 = bf16[1024,512]{1,0:T(8,128)(2,1)} custom-call(f32[1024,512]{1,0:T(8,128)S(1)} %get-tuple-element.23.mixed, f32[8,8,128]{2,1,0:T(8,128)S(1)} %all_to_all.17.squares, f32[1,512]{1,0:T(1,128)S(1)} %bitcast.5), custom_call_target="tpu_custom_call" | custom-call | tf_op jit(solution)/shard_map/scored/pallas_call | solution.py:242
  (1 shorter events, 0.0 us)
Async XLA Ops:
  0.0 59.7 %copy-start.1 = (bf16[1024,512]{1,0:T(8,128)(2,1)S(1)}, bf16[1024,512]{1,0:T(8,128)(2,1)}, u32[]{:S(2)}) copy-start(bf16[1024,512]{1,0:T(8,128)(2,1)} %values.3) | copy-start | bytes 3145732
  0.0 59.7 %copy-start = (bf16[1024,512]{1,0:T(8,128)(2,1)S(1)}, bf16[1024,512]{1,0:T(8,128)(2,1)}, u32[]{:S(2)}) copy-start(bf16[1024,512]{1,0:T(8,128)(2,1)} %keys.3) | copy-start | bytes 3145732
  0.0 59.7 %copy-start.3 = (bf16[1024,512]{1,0:T(8,128)(2,1)S(1)}, bf16[1024,512]{1,0:T(8,128)(2,1)}, u32[]{:S(2)}) copy-start(bf16[1024,512]{1,0:T(8,128)(2,1)} %queries.1) | copy-start | bytes 3145732
  19.0 4.6 %collective-permute-start = (f32[4,32,128]{2,1,0:T(8,128)S(1)}, f32[4,32,128]{2,1,0:T(8,128)S(1)}, u32[]{:S(2)}, u32[]{:S(2)}) collective-permute-start(f32[4,32,128]{2,1,0:T(8,128)S(1)} %get-tuple-element.15), channel_id=1, source_target_pairs={{64,0},{72,8},{80,16},{88,24},{192,128},{200,136},{208,144},{216,1... | collective-permute-start | bytes 196616 | tf_op jit(solution)/shard_map/ppermute | solution.py:154
  19.7 10.9 %collective-permute-start.1 = (f32[4,32,128]{2,1,0:T(8,128)S(1)}, f32[4,32,128]{2,1,0:T(8,128)S(1)}, u32[]{:S(2)}, u32[]{:S(2)}) collective-permute-start(f32[4,32,128]{2,1,0:T(8,128)S(1)} %get-tuple-element.16), channel_id=1, source_target_pairs={{96,0},{104,8},{112,16},{120,24},{224,128},{232,136},{240,144},{24... | collective-permute-start | bytes 196616 | tf_op jit(solution)/shard_map/ppermute | solution.py:154
  21.0 10.3 %collective-permute-start.2 = (f32[4,32,128]{2,1,0:T(8,128)S(1)}, f32[4,32,128]{2,1,0:T(8,128)S(1)}, u32[]{:S(2)}, u32[]{:S(2)}) collective-permute-start(f32[4,32,128]{2,1,0:T(8,128)S(1)} %get-tuple-element.17), channel_id=1, source_target_pairs={{32,0},{0,32},{40,8},{8,40},{48,16},{16,48},{56,24},{24,56},{160,1... | collective-permute-start | bytes 196616 | tf_op jit(solution)/shard_map/ppermute | solution.py:154
  21.6 12.1 %collective-permute-start.3 = (f32[4,32,128]{2,1,0:T(8,128)S(1)}, f32[4,32,128]{2,1,0:T(8,128)S(1)}, u32[]{:S(2)}, u32[]{:S(2)}) collective-permute-start(f32[4,32,128]{2,1,0:T(8,128)S(1)} %get-tuple-element.18), channel_id=1, source_target_pairs={{0,96},{8,104},{16,112},{24,120},{128,224},{136,232},{144,240},{15... | collective-permute-start | bytes 196616 | tf_op jit(solution)/shard_map/ppermute | solution.py:154
  22.9 10.8 %collective-permute-start.4 = (f32[4,32,128]{2,1,0:T(8,128)S(1)}, f32[4,32,128]{2,1,0:T(8,128)S(1)}, u32[]{:S(2)}, u32[]{:S(2)}) collective-permute-start(f32[4,32,128]{2,1,0:T(8,128)S(1)} %get-tuple-element.19), channel_id=1, source_target_pairs={{0,64},{64,32},{8,72},{72,40},{16,80},{80,48},{24,88},{88,56},{128... | collective-permute-start | bytes 196616 | tf_op jit(solution)/shard_map/ppermute | solution.py:154
  23.6 17.0 %collective-permute-start.5 = (f32[4,32,128]{2,1,0:T(8,128)S(1)}, f32[4,32,128]{2,1,0:T(8,128)S(1)}, u32[]{:S(2)}, u32[]{:S(2)}) collective-permute-start(f32[4,32,128]{2,1,0:T(8,128)S(1)} %get-tuple-element.20), channel_id=1, source_target_pairs={{32,96},{96,32},{40,104},{104,40},{48,112},{112,48},{56,120},{120,... | collective-permute-start | bytes 196616 | tf_op jit(solution)/shard_map/ppermute | solution.py:154
  30.6 10.0 %collective-permute-start.6 = (f32[4,32,128]{2,1,0:T(8,128)S(1)}, f32[4,32,128]{2,1,0:T(8,128)S(1)}, u32[]{:S(2)}, u32[]{:S(2)}) collective-permute-start(f32[4,32,128]{2,1,0:T(8,128)S(1)} %get-tuple-element.21), channel_id=1, source_target_pairs={{32,64},{40,72},{48,80},{56,88},{160,192},{168,200},{176,208},{184... | collective-permute-start | bytes 196616 | tf_op jit(solution)/shard_map/ppermute | solution.py:154
  31.3 11.0 %collective-permute-start.7 = (f32[4,32,128]{2,1,0:T(8,128)S(1)}, f32[4,32,128]{2,1,0:T(8,128)S(1)}, u32[]{:S(2)}, u32[]{:S(2)}) collective-permute-start(f32[4,32,128]{2,1,0:T(8,128)S(1)} %get-tuple-element.22), channel_id=1, source_target_pairs={{64,96},{96,64},{72,104},{104,72},{80,112},{112,80},{88,120},{120,... | collective-permute-start | bytes 196616 | tf_op jit(solution)/shard_map/ppermute | solution.py:154
  59.7 13.1 %copy-start.2 = (f32[512]{0:T(512)S(1)}, f32[512]{0:T(512)}, u32[]{:S(2)}) copy-start(f32[512]{0:T(512)} %param.7) | copy-start | bytes 6148

commit v4 on v3

--- a/solution.py
+++ b/solution.py
@@ -20,6 +20,7 @@
 VMEM = pl.BlockSpec(memory_space=pltpu.VMEM)
 HBM = pl.BlockSpec(memory_space=pltpu.HBM)
 STATE_MIB = 53.2
+LOCAL_MIB = 32
 MIXED_MIB = 32
 OTHER_MIB = 32
 
@@ -113,7 +114,7 @@
             out[x] = run
 
 
-def back_kernel(got, *rest):
+def back_kernel(meanwhile, got, *rest):
     parts, back = rest[:-1], rest[-1]
     mine = (lax.axis_index("ctx") // NEAR) % FAR
     run = None
@@ -139,7 +140,7 @@
             run = run + got[x * NEAR + b]
 
 
-def exclusive_states(state):
+def exclusive_states(state, meanwhile):
     rows = state.shape[0] * HD // MEMBERS
     pieces = state.reshape(MEMBERS, rows, HD)
     got = lax.all_to_all(pieces, "ctx", 0, 0, axis_index_groups=near_groups())
@@ -154,68 +155,93 @@
     parts = [lax.ppermute(out, "ctx", between(step)) for out, step in zip(sent, STEPS)]
     back = pl.pallas_call(
         back_kernel,
-        in_specs=[VMEM] * (1 + len(parts)),
+        in_specs=[HBM] + [VMEM] * (1 + len(parts)),
         out_specs=VMEM,
         out_shape=jax.ShapeDtypeStruct(got.shape, jnp.float32),
         compiler_params=grant(OTHER_MIB),
         name="back",
-    )(got, *parts)
+    )(meanwhile, got, *parts)
     mine = lax.all_to_all(back, "ctx", 0, 0, axis_index_groups=near_groups())
     return mine.reshape(state.shape)
 
 
-def mixed_kernel(queries, keys, values, prefix, mixed, squares):
+def local_kernel(queries, keys, values, out, first, top_queries):
     half = BLOCK // 2
-    tiles = BLOCK // HD
     row = lax.broadcasted_iota(jnp.int32, (half, half), 0)
     col = lax.broadcasted_iota(jnp.int32, (half, half), 1)
     lower = row >= col
-    for start in range(0, queries.shape[0], BLOCK):
-        top_rows = slice(start, start + half)
-        low_rows = slice(start + half, start + BLOCK)
-        acc = [None, None]
-        for h in range(queries.shape[1] // HD):
-            cols = head_columns(h)
-            state = prefix[h]
-            if start:
-                state = state + contract_tokens(keys[:start, cols], values[:start, cols])
-            state = state.astype(jnp.bfloat16)
+    top_queries[...] = queries[:BLOCK]
+    for h in range(queries.shape[1] // HD):
+        cols = head_columns(h)
+        first[h] = contract_tokens(keys[:BLOCK, cols], values[:BLOCK, cols])
+        for start in range(0, queries.shape[0], BLOCK):
+            top_rows = slice(start, start + half)
+            low_rows = slice(start + half, start + BLOCK)
             q, k = queries[top_rows, cols], keys[top_rows, cols]
             top = jnp.where(lower, contract_last(q, k), 0.0).astype(jnp.bfloat16)
-            m = jnp.dot(q, state, preferred_element_type=jnp.float32)
-            m = m + jnp.dot(top, values[top_rows, cols], preferred_element_type=jnp.float32)
-            mixed[top_rows, cols] = m
-            acc[0] = m * m if h == 0 else acc[0] + m * m
+            out[top_rows, cols] = jnp.dot(top, values[top_rows, cols], preferred_element_type=jnp.float32)
             q = queries[low_rows, cols]
             side = contract_last(q, k).astype(jnp.bfloat16)
             low = jnp.where(lower, contract_last(q, keys[low_rows, cols]), 0.0).astype(jnp.bfloat16)
             both = jnp.concatenate([side, low], axis=1)
-            m = jnp.dot(q, state, preferred_element_type=jnp.float32)
-            m = m + jnp.dot(both, values[start : start + BLOCK, cols], preferred_element_type=jnp.float32)
-            mixed[low_rows, cols] = m
-            acc[1] = m * m if h == 0 else acc[1] + m * m
-        for i, a in enumerate(acc):
-            turned = jnp.swapaxes(a.reshape(tiles // 2, HD, HD), 1, 2)
-            sums = jnp.sum(turned, axis=1)
-            at = start // HD + i * (tiles // 2)
-            for p in range(PEERS):
-                squares[p, at : at + tiles // 2] = sums
-
-
-def mixed_part(queries, keys, values, prefix):
+            v = values[start : start + BLOCK, cols]
+            out[low_rows, cols] = jnp.dot(both, v, preferred_element_type=jnp.float32)
+
+
+def local_part(queries, keys, values):
     rows, width = queries.shape
     return pl.pallas_call(
+        local_kernel,
+        in_specs=[VMEM] * 3,
+        out_specs=[VMEM] * 3,
+        out_shape=[
+            jax.ShapeDtypeStruct((rows, width), jnp.float32),
+            jax.ShapeDtypeStruct((width // HD, HD, HD), jnp.float32),
+            jax.ShapeDtypeStruct((BLOCK, width), queries.dtype),
+        ],
+        compiler_params=grant(LOCAL_MIB),
+        cost_estimate=pl.CostEstimate(flops=4 * rows * BLOCK * width, bytes_accessed=10 * rows * width, transcendentals=0),
+        name="local",
+    )(queries, keys, values)
+
+
+def mixed_kernel(queries, top_queries, local, prefix, first, mixed, squares, held, sem):
+    tiles = BLOCK // HD
+    rest = pltpu.make_async_copy(queries.at[pl.ds(BLOCK, BLOCK)], held, sem)
+    rest.start()
+    for i in range(local.shape[0] // BLOCK):
+        if i:
+            rest.wait()
+        rows = slice(i * BLOCK, (i + 1) * BLOCK)
+        acc = None
+        for h in range(local.shape[1] // HD):
+            cols = head_columns(h)
+            state = prefix[h] + first[h] if i else prefix[h]
+            q = held[:, cols] if i else top_queries[:, cols]
+            m = jnp.dot(q, state.astype(jnp.bfloat16), preferred_element_type=jnp.float32) + local[rows, cols]
+            mixed[rows, cols] = m
+            acc = m * m if h == 0 else acc + m * m
+        turned = jnp.swapaxes(acc.reshape(tiles, HD, HD), 1, 2)
+        sums = jnp.sum(turned, axis=1)
+        for p in range(PEERS):
+            squares[p, i * tiles : (i + 1) * tiles] = sums
+
+
+def mixed_part(queries, top_queries, local, prefix, first):
+    rows, width = queries.shape
+    return pl.pallas_call(
         mixed_kernel,
-        in_specs=[VMEM] * 4,
+        in_specs=[HBM] + [VMEM] * 4,
         out_specs=[VMEM] * 2,
         out_shape=[
             jax.ShapeDtypeStruct((rows, width), jnp.float32),
             jax.ShapeDtypeStruct((PEERS, rows // HD, HD), jnp.float32),
         ],
+        scratch_shapes=[pltpu.VMEM((BLOCK, width), queries.dtype), pltpu.SemaphoreType.DMA(())],
         compiler_params=grant(MIXED_MIB),
-        cost_estimate=pl.CostEstimate(flops=4 * rows * BLOCK * width, bytes_accessed=10 * rows * width, transcendentals=0),
+        cost_estimate=pl.CostEstimate(flops=2 * rows * HD * width, bytes_accessed=10 * rows * width, transcendentals=0),
         name="mixed",
-    )(queries, keys, values, prefix)
+    )(queries, top_queries, local, prefix, first)
 
 
 def scored_kernel(mixed, squares, gain, out, rows, sems):
@@ -252,8 +278,9 @@
 
 def shards(queries, keys, values, gain):
     total = shard_state(keys, values)
-    prefix = exclusive_states(total)
-    mixed, squares = mixed_part(queries, keys, values, prefix)
+    local, first, top_queries = local_part(queries, keys, values)
+    prefix = exclusive_states(total, first)
+    mixed, squares = mixed_part(queries, top_queries, local, prefix, first)
     squares = lax.all_to_all(squares, "tp", 0, 0)
     return scored_part(mixed, squares, gain)
 

time: 74.2 us -> 71.7 us (0.966)
  waiting for transfers between devices: 8.56 us -> 6.01 us
    ppermute x8, waiting for transfers between devices: 8.56 us -> 6.01 us  [exclusive_states(): lax.ppermute(out, 'ctx', between(step))]
    pallas_call x2 -> x3, Pallas kernels: 3.43 us -> 3.38 us  [the longest x1 2.51 us: local_part(): pl.pallas_call(local_kernel, in_specs=[VMEM] * 3, out_specs=[VMEM] * 3, o...]
  transfers between devices with their start and end apart: 8 -> 8, of which waited for: 2 -> 2; matrix products, arithmetic and copies ran while one was open for 0% -> 0% of each run, Pallas kernels for 0% -> 4%
where the time goes in v4:
time: 71.7 us; the launch traced here: 71.4 us
  blocking collectives  43.4 us (61%)
  starting transfers between devices  14.7 us (21%)
  Pallas kernels  7.05 us (10%)
  waiting for transfers between devices  6.01 us (8%)
    all_to_all x1, blocking collectives, exclusive_states(): mine = lax.all_to_all(back, 'ctx', 0, 0, axis_index_groups=near_groups())  17.3 us
    all_to_all x1, blocking collectives, exclusive_states(): got = lax.all_to_all(pieces, 'ctx', 0, 0, axis_index_groups=near_groups())  16.5 us
    ppermute x8, starting transfers between devices, exclusive_states(): lax.ppermute(out, 'ctx', between(step))  14.7 us
    all_to_all x1, blocking collectives, shards(): squares = lax.all_to_all(squares, 'tp', 0, 0)  9.71 us
    ppermute x8, waiting for transfers between devices, exclusive_states(): lax.ppermute(out, 'ctx', between(step))  6.01 us
    pallas_call x1, Pallas kernels, local_part(): pl.pallas_call(local_kernel, in_specs=[VMEM] * 3, out_specs=[VMEM] * 3, o...  2.51 us
    pallas_call x1, Pallas kernels, shard_state(): pl.pallas_call(state_kernel, in_specs=[HBM, HBM], out_specs=VMEM, out_sha...  2.47 us
  transfers between devices with their start and end apart: 8, of which 2 were waited for; matrix products, arithmetic and copies ran while one was open for 0% of the time, Pallas kernels for 4%

profile of v4, /device:TPU:384, one launch (start us, length us, event | category | flops | bytes accessed | tf_op | source)
XLA Modules:
  0.0 71.4 jit_solution(14920506144619711767)
XLA Ops:
  0.0 0.0 copy-start.1
  0.0 0.0 copy-start
  0.0 0.0 copy-start.2
  0.0 2.5 %states.1 = f32[4,128,128]{2,1,0:T(8,128)S(1)} custom-call(bf16[1024,512]{1,0:T(8,128)(2,1)} %keys.3, bf16[1024,512]{1,0:T(8,128)(2,1)} %values.3), custom_call_target="tpu_custom_call" | custom-call | flops 134217728 | bytes 2097152 | tf_op jit(solution)/shard_map/states/pallas_call | solution.py:80
  2.5 16.5 %all_to_all.15.got = f32[16,32,128]{2,1,0:T(8,128)S(1)} all-to-all(f32[16,32,128]{2,1,0:T(8,128)S(1)} %bitcast.4), channel_id=1, replica_groups={{0,8,16,24,128,136,144,152,256,264,272,280,384,392,400,408},{32,40,48,5..., dimensions={0} | all-to-all | bytes 524288 | tf_op jit(solution)/shard_map/all_to_all | solution.py:146
  19.0 0.7 collective-permute-start
  19.7 1.3 %collective-permute-start.1 = (f32[4,32,128]{2,1,0:T(8,128)S(1)}, f32[4,32,128]{2,1,0:T(8,128)S(1)}, u32[]{:S(2)}, u32[]{:S(2)}) collective-permute-start(f32[4,32,128]{2,1,0:T(8,128)S(1)} %get-tuple-element.22), channel_id=1, source_target_pairs={{96,0},{104,8},{112,16},{120,24},{224,128},{232,136},{240,144},{24... | collective-permute-start | bytes 196616 | tf_op jit(solution)/shard_map/ppermute | solution.py:155
  21.0 0.7 collective-permute-start.2
  21.6 1.3 %collective-permute-start.3 = (f32[4,32,128]{2,1,0:T(8,128)S(1)}, f32[4,32,128]{2,1,0:T(8,128)S(1)}, u32[]{:S(2)}, u32[]{:S(2)}) collective-permute-start(f32[4,32,128]{2,1,0:T(8,128)S(1)} %get-tuple-element.24), channel_id=1, source_target_pairs={{0,96},{8,104},{16,112},{24,120},{128,224},{136,232},{144,240},{15... | collective-permute-start | bytes 196616 | tf_op jit(solution)/shard_map/ppermute | solution.py:155
  22.9 0.7 collective-permute-start.4
  23.6 0.0 collective-permute-done.rest_0_
  23.6 7.0 %collective-permute-start.5 = (f32[4,32,128]{2,1,0:T(8,128)S(1)}, f32[4,32,128]{2,1,0:T(8,128)S(1)}, u32[]{:S(2)}, u32[]{:S(2)}) collective-permute-start(f32[4,32,128]{2,1,0:T(8,128)S(1)} %get-tuple-element.26), channel_id=1, source_target_pairs={{32,96},{96,32},{40,104},{104,40},{48,112},{112,48},{56,120},{120,... | collective-permute-start | bytes 196616 | tf_op jit(solution)/shard_map/ppermute | solution.py:155
  30.6 0.0 collective-permute-done.1.rest_1_
  30.6 0.7 collective-permute-start.6
  31.3 0.0 collective-permute-done.2.rest_2_
  31.3 2.5 %collective-permute-start.7 = (f32[4,32,128]{2,1,0:T(8,128)S(1)}, f32[4,32,128]{2,1,0:T(8,128)S(1)}, u32[]{:S(2)}, u32[]{:S(2)}) collective-permute-start(f32[4,32,128]{2,1,0:T(8,128)S(1)} %get-tuple-element.28), channel_id=1, source_target_pairs={{64,96},{96,64},{72,104},{104,72},{80,112},{112,80},{88,120},{120,... | collective-permute-start | bytes 196616 | tf_op jit(solution)/shard_map/ppermute | solution.py:155
  33.8 0.0 copy-done.1
  33.8 0.0 copy-done
  33.8 0.0 copy-done.2
  33.8 2.5 %local.1 = (f32[1024,512]{1,0:T(8,128)S(1)}, f32[4,128,128]{2,1,0:T(8,128)S(1)}, bf16[512,512]{1,0:T(8,128)(2,1)S(1)}) custom-call(bf16[1024,512]{1,0:T(8,128)(2,1)S(1)} %copy-done.2, bf16[1024,512]{1,0:T(8,128)(2,1)S(1)} %copy-done, bf16[1024,512]{1,0:T(8,128)(2,1)S(1)} %copy-done.1), custom_call_target="tpu_custom_call" | custom-call | flops 1073741824 | bytes 5242880 | tf_op jit(solution)/shard_map/local/pallas_call | solution.py:193
  36.3 0.0 collective-permute-done.3.rest_3_
  36.3 0.0 collective-permute-done.4.rest_4_
  36.3 4.3 %collective-permute-done.5.rest_5_ = f32[4,32,128]{2,1,0:T(8,128)S(1)} collective-permute-done((f32[4,32,128]{2,1,0:T(8,128)S(1)}, f32[4,32,128]{2,1,0:T(8,128)S(1)}, u32[]{:S(2)}, u32[]{:S(2)}) %collective-permute-start.5) | collective-permute-done | bytes 65568 | tf_op jit(solution)/shard_map/ppermute | solution.py:155
  40.6 0.0 collective-permute-done.6.rest_6_
  40.6 1.7 %collective-permute-done.7.rest_7_ = f32[4,32,128]{2,1,0:T(8,128)S(1)} collective-permute-done((f32[4,32,128]{2,1,0:T(8,128)S(1)}, f32[4,32,128]{2,1,0:T(8,128)S(1)}, u32[]{:S(2)}, u32[]{:S(2)}) %collective-permute-start.7) | collective-permute-done | bytes 65568 | tf_op jit(solution)/shard_map/ppermute | solution.py:155
  42.3 0.1 back.1
  42.4 17.3 %all_to_all.16 = f32[16,32,128]{2,1,0:T(8,128)S(1)} all-to-all(f32[16,32,128]{2,1,0:T(8,128)S(1)} %back.1), channel_id=1, replica_groups={{0,8,16,24,128,136,144,152,256,264,272,280,384,392,400,408},{32,40,48,5..., dimensions={0} | all-to-all | bytes 524288 | tf_op jit(solution)/shard_map/all_to_all | solution.py:164
  59.7 0.0 copy-start.3
  59.7 0.8 %mixed.1 = (f32[1024,512]{1,0:T(8,128)S(1)}, f32[8,8,128]{2,1,0:T(8,128)S(1)}) custom-call(bf16[1024,512]{1,0:T(8,128)(2,1)S(1)} %copy-done.2, bf16[512,512]{1,0:T(8,128)(2,1)S(1)} %get-tuple-element.18.top_queries, f32[1024,512]{1,0:T(8,128)S(1)} %get-tuple-element.19.local, f32[4,128,128]{2,1,0:T(8,128)S(1)} %bitcast.3, ...), custom_call_target="tpu_custom_call" | custom-call | flops 134217728 | bytes 5242880 | tf_op jit(solution)/shard_map/mixed/pallas_call | solution.py:232
  60.5 9.7 %all_to_all.17.squares = f32[8,8,128]{2,1,0:T(8,128)S(1)} all-to-all(f32[8,8,128]{2,1,0:T(8,128)S(1)} %get-tuple-element.30), channel_id=1, replica_groups=mesh['ctx'=64,'tp'=8] {'tp'}, dimensions={0} | all-to-all | bytes 65536 | tf_op jit(solution)/shard_map/all_to_all | solution.py:284
  70.2 0.0 copy-done.3
  70.2 1.2 %scored.1 = bf16[1024,512]{1,0:T(8,128)(2,1)} custom-call(f32[1024,512]{1,0:T(8,128)S(1)} %get-tuple-element.29.mixed, f32[8,8,128]{2,1,0:T(8,128)S(1)} %all_to_all.17.squares, f32[1,512]{1,0:T(1,128)S(1)} %bitcast.5), custom_call_target="tpu_custom_call" | custom-call | tf_op jit(solution)/shard_map/scored/pallas_call | solution.py:268
  (1 shorter events, 0.0 us)
Async XLA Ops:
  0.0 33.8 %copy-start.1 = (bf16[1024,512]{1,0:T(8,128)(2,1)S(1)}, bf16[1024,512]{1,0:T(8,128)(2,1)}, u32[]{:S(2)}) copy-start(bf16[1024,512]{1,0:T(8,128)(2,1)} %values.3) | copy-start | bytes 3145732
  0.0 33.8 %copy-start = (bf16[1024,512]{1,0:T(8,128)(2,1)S(1)}, bf16[1024,512]{1,0:T(8,128)(2,1)}, u32[]{:S(2)}) copy-start(bf16[1024,512]{1,0:T(8,128)(2,1)} %keys.3) | copy-start | bytes 3145732
  0.0 33.8 %copy-start.2 = (bf16[1024,512]{1,0:T(8,128)(2,1)S(1)}, bf16[1024,512]{1,0:T(8,128)(2,1)}, u32[]{:S(2)}) copy-start(bf16[1024,512]{1,0:T(8,128)(2,1)} %queries.3) | copy-start | bytes 3145732
  19.0 4.6 %collective-permute-start = (f32[4,32,128]{2,1,0:T(8,128)S(1)}, f32[4,32,128]{2,1,0:T(8,128)S(1)}, u32[]{:S(2)}, u32[]{:S(2)}) collective-permute-start(f32[4,32,128]{2,1,0:T(8,128)S(1)} %get-tuple-element.21), channel_id=1, source_target_pairs={{64,0},{72,8},{80,16},{88,24},{192,128},{200,136},{208,144},{216,1... | collective-permute-start | bytes 196616 | tf_op jit(solution)/shard_map/ppermute | solution.py:155
  19.7 10.9 %collective-permute-start.1 = (f32[4,32,128]{2,1,0:T(8,128)S(1)}, f32[4,32,128]{2,1,0:T(8,128)S(1)}, u32[]{:S(2)}, u32[]{:S(2)}) collective-permute-start(f32[4,32,128]{2,1,0:T(8,128)S(1)} %get-tuple-element.22), channel_id=1, source_target_pairs={{96,0},{104,8},{112,16},{120,24},{224,128},{232,136},{240,144},{24... | collective-permute-start | bytes 196616 | tf_op jit(solution)/shard_map/ppermute | solution.py:155
  21.0 10.3 %collective-permute-start.2 = (f32[4,32,128]{2,1,0:T(8,128)S(1)}, f32[4,32,128]{2,1,0:T(8,128)S(1)}, u32[]{:S(2)}, u32[]{:S(2)}) collective-permute-start(f32[4,32,128]{2,1,0:T(8,128)S(1)} %get-tuple-element.23), channel_id=1, source_target_pairs={{32,0},{0,32},{40,8},{8,40},{48,16},{16,48},{56,24},{24,56},{160,1... | collective-permute-start | bytes 196616 | tf_op jit(solution)/shard_map/ppermute | solution.py:155
  21.6 14.7 %collective-permute-start.3 = (f32[4,32,128]{2,1,0:T(8,128)S(1)}, f32[4,32,128]{2,1,0:T(8,128)S(1)}, u32[]{:S(2)}, u32[]{:S(2)}) collective-permute-start(f32[4,32,128]{2,1,0:T(8,128)S(1)} %get-tuple-element.24), channel_id=1, source_target_pairs={{0,96},{8,104},{16,112},{24,120},{128,224},{136,232},{144,240},{15... | collective-permute-start | bytes 196616 | tf_op jit(solution)/shard_map/ppermute | solution.py:155
  22.9 13.4 %collective-permute-start.4 = (f32[4,32,128]{2,1,0:T(8,128)S(1)}, f32[4,32,128]{2,1,0:T(8,128)S(1)}, u32[]{:S(2)}, u32[]{:S(2)}) collective-permute-start(f32[4,32,128]{2,1,0:T(8,128)S(1)} %get-tuple-element.25), channel_id=1, source_target_pairs={{0,64},{64,32},{8,72},{72,40},{16,80},{80,48},{24,88},{88,56},{128... | collective-permute-start | bytes 196616 | tf_op jit(solution)/shard_map/ppermute | solution.py:155
  23.6 17.0 %collective-permute-start.5 = (f32[4,32,128]{2,1,0:T(8,128)S(1)}, f32[4,32,128]{2,1,0:T(8,128)S(1)}, u32[]{:S(2)}, u32[]{:S(2)}) collective-permute-start(f32[4,32,128]{2,1,0:T(8,128)S(1)} %get-tuple-element.26), channel_id=1, source_target_pairs={{32,96},{96,32},{40,104},{104,40},{48,112},{112,48},{56,120},{120,... | collective-permute-start | bytes 196616 | tf_op jit(solution)/shard_map/ppermute | solution.py:155
  30.6 10.0 %collective-permute-start.6 = (f32[4,32,128]{2,1,0:T(8,128)S(1)}, f32[4,32,128]{2,1,0:T(8,128)S(1)}, u32[]{:S(2)}, u32[]{:S(2)}) collective-permute-start(f32[4,32,128]{2,1,0:T(8,128)S(1)} %get-tuple-element.27), channel_id=1, source_target_pairs={{32,64},{40,72},{48,80},{56,88},{160,192},{168,200},{176,208},{184... | collective-permute-start | bytes 196616 | tf_op jit(solution)/shard_map/ppermute | solution.py:155
  31.3 11.0 %collective-permute-start.7 = (f32[4,32,128]{2,1,0:T(8,128)S(1)}, f32[4,32,128]{2,1,0:T(8,128)S(1)}, u32[]{:S(2)}, u32[]{:S(2)}) collective-permute-start(f32[4,32,128]{2,1,0:T(8,128)S(1)} %get-tuple-element.28), channel_id=1, source_target_pairs={{64,96},{96,64},{72,104},{104,72},{80,112},{112,80},{88,120},{120,... | collective-permute-start | bytes 196616 | tf_op jit(solution)/shard_map/ppermute | solution.py:155
  59.7 10.5 %copy-start.3 = (f32[512]{0:T(512)S(1)}, f32[512]{0:T(512)}, u32[]{:S(2)}) copy-start(f32[512]{0:T(512)} %param.7) | copy-start | bytes 6148

commit v5 on v4

--- a/solution.py
+++ b/solution.py
@@ -1,3 +1,5 @@
+import functools
+
 import jax
 import jax.numpy as jnp
 from jax import lax
@@ -21,6 +23,7 @@
 HBM = pl.BlockSpec(memory_space=pltpu.HBM)
 STATE_MIB = 53.2
 LOCAL_MIB = 32
+EARLY = 1
 MIXED_MIB = 32
 OTHER_MIB = 32
 
@@ -95,14 +98,27 @@
 
 STEPS = (
     ((2, 0),),
-    ((3, 0),),
-    ((1, 0), (0, 1)),
-    ((0, 3),),
-    ((0, 2), (2, 1)),
-    ((1, 3), (3, 1)),
+    ((1, 0), (2, 1),),
+    ((3, 0), (0, 3),),
+    ((0, 1), (2, 3),),
+    ((3, 1), (1, 3),),
     ((1, 2),),
-    ((2, 3), (3, 2)),
+    ((3, 2),),
 )
+RELAY = len(STEPS) - 1
+CARRIED = 2
+WITH = (0, 1)
+LOCAL_AFTER = 1
+
+
+def relay_kernel(own, *rest):
+    carried, out = rest[len(WITH)], rest[-1]
+    src, dst = STEPS[RELAY][0]
+    for x in range(XS):
+        if src < dst:
+            out[x] = own[x] + carried[x]
+        else:
+            out[x] = own[x - 1] + carried[x] if x else carried[x]
 
 
 def own_kernel(got, *outs):
@@ -121,8 +137,8 @@
     for x in range(XS):
         start = jnp.zeros(got.shape[1:], jnp.float32) if run is None else run
         run = start
-        for step, part in zip(STEPS, parts):
-            shifted = [dst for src, dst in step if src > dst]
+        for k, (step, part) in enumerate(zip(STEPS, parts)):
+            shifted = [dst for src, dst in step if src > dst and k != RELAY]
             if not shifted:
                 start = start + part[x]
             elif len(shifted) == len(step):
@@ -140,7 +156,7 @@
             run = run + got[x * NEAR + b]
 
 
-def exclusive_states(state, meanwhile):
+def exclusive_states(state, local):
     rows = state.shape[0] * HD // MEMBERS
     pieces = state.reshape(MEMBERS, rows, HD)
     got = lax.all_to_all(pieces, "ctx", 0, 0, axis_index_groups=near_groups())
@@ -152,7 +168,22 @@
         compiler_params=grant(OTHER_MIB),
         name="sent",
     )(got)
-    parts = [lax.ppermute(out, "ctx", between(step)) for out, step in zip(sent, STEPS)]
+    parts = []
+    for k, step in enumerate(STEPS):
+        out = sent[k]
+        if k == RELAY:
+            held = local(parts[LOCAL_AFTER])
+            late = [parts[j] for j in (*WITH, CARRIED)] + [held[1]]
+            out = pl.pallas_call(
+                relay_kernel,
+                in_specs=[VMEM] * len(late) + [HBM],
+                out_specs=VMEM,
+                out_shape=jax.ShapeDtypeStruct(out.shape, jnp.float32),
+                compiler_params=grant(OTHER_MIB),
+                name="relay",
+            )(out, *late)
+        parts.append(lax.ppermute(out, "ctx", between(step)))
+    held = local(out, held)
     back = pl.pallas_call(
         back_kernel,
         in_specs=[HBM] + [VMEM] * (1 + len(parts)),
@@ -160,12 +191,21 @@
         out_shape=jax.ShapeDtypeStruct(got.shape, jnp.float32),
         compiler_params=grant(OTHER_MIB),
         name="back",
-    )(meanwhile, got, *parts)
+    )(held[1], got, *parts)
     mine = lax.all_to_all(back, "ctx", 0, 0, axis_index_groups=near_groups())
-    return mine.reshape(state.shape)
-
-
-def local_kernel(queries, keys, values, out, first, top_queries):
+    return mine.reshape(state.shape), held
+
+
+def local_kernel(early, queries, keys, values, *rest):
+    out, first, top_queries = rest[-3:]
+    leading = (lax.axis_index("ctx") // NEAR) % FAR < EARLY
+
+    @pl.when(leading == early)
+    def _():
+        local_work(queries, keys, values, out, first, top_queries)
+
+
+def local_work(queries, keys, values, out, first, top_queries):
     half = BLOCK // 2
     row = lax.broadcasted_iota(jnp.int32, (half, half), 0)
     col = lax.broadcasted_iota(jnp.int32, (half, half), 1)
@@ -188,21 +228,23 @@
             out[low_rows, cols] = jnp.dot(both, v, preferred_element_type=jnp.float32)
 
 
-def local_part(queries, keys, values):
+def local_part(queries, keys, values, after, held=None):
     rows, width = queries.shape
+    more = [after] + (list(held) if held else [])
     return pl.pallas_call(
-        local_kernel,
-        in_specs=[VMEM] * 3,
+        functools.partial(local_kernel, held is None),
+        in_specs=[VMEM] * 3 + [HBM] + [VMEM] * (len(more) - 1),
         out_specs=[VMEM] * 3,
         out_shape=[
             jax.ShapeDtypeStruct((rows, width), jnp.float32),
             jax.ShapeDtypeStruct((width // HD, HD, HD), jnp.float32),
             jax.ShapeDtypeStruct((BLOCK, width), queries.dtype),
         ],
+        input_output_aliases={4 + i: i for i in range(3)} if held else {},
         compiler_params=grant(LOCAL_MIB),
         cost_estimate=pl.CostEstimate(flops=4 * rows * BLOCK * width, bytes_accessed=10 * rows * width, transcendentals=0),
         name="local",
-    )(queries, keys, values)
+    )(queries, keys, values, *more)
 
 
 def mixed_kernel(queries, top_queries, local, prefix, first, mixed, squares, held, sem):
@@ -278,8 +320,7 @@
 
 def shards(queries, keys, values, gain):
     total = shard_state(keys, values)
-    local, first, top_queries = local_part(queries, keys, values)
-    prefix = exclusive_states(total, first)
+    prefix, (local, first, top_queries) = exclusive_states(total, functools.partial(local_part, queries, keys, values))
     mixed, squares = mixed_part(queries, top_queries, local, prefix, first)
     squares = lax.all_to_all(squares, "tp", 0, 0)
     return scored_part(mixed, squares, gain)

time: 71.7 us -> 68.9 us (0.961)
  the two profiles are of different devices: /device:TPU:384 before, /device:TPU:128 now
where the time goes in v5:
time: 68.9 us; the launch traced here: 68.6 us
  blocking collectives  43.3 us (63%)
  starting transfers between devices  14.8 us (21%)
  Pallas kernels  7.1 us (10%)
  waiting for transfers between devices  3.28 us (5%)
    all_to_all x1, blocking collectives, exclusive_states(): got = lax.all_to_all(pieces, 'ctx', 0, 0, axis_index_groups=near_groups())  19.1 us
    ppermute x7, starting transfers between devices, exclusive_states(): parts.append(lax.ppermute(out, 'ctx', between(step)))  14.8 us
    all_to_all x1, blocking collectives, exclusive_states(): mine = lax.all_to_all(back, 'ctx', 0, 0, axis_index_groups=near_groups())  14.4 us
    all_to_all x1, blocking collectives, shards(): squares = lax.all_to_all(squares, 'tp', 0, 0)  9.72 us
    ppermute x7, waiting for transfers between devices, exclusive_states(): parts.append(lax.ppermute(out, 'ctx', between(step)))  3.28 us
    pallas_call x2, Pallas kernels, local_part(): pl.pallas_call(functools.partial(local_kernel, held is None), in_specs=[V...  2.56 us
    pallas_call x1, Pallas kernels, shard_state(): pl.pallas_call(state_kernel, in_specs=[HBM, HBM], out_specs=VMEM, out_sha...  2.47 us
  transfers between devices with their start and end apart: 7, of which 2 were waited for; matrix products, arithmetic and copies ran while one was open for 0% of the time, Pallas kernels for 4%

profile of v5, /device:TPU:128, one launch (start us, length us, event | category | flops | bytes accessed | tf_op | source)
XLA Modules:
  0.0 68.6 jit_solution(13797280562485554054)
XLA Ops:
  0.0 0.0 copy-start.1
  0.0 0.0 copy-start
  0.0 0.0 copy-start.2
  0.0 2.5 %states.1 = f32[4,128,128]{2,1,0:T(8,128)S(1)} custom-call(bf16[1024,512]{1,0:T(8,128)(2,1)} %keys.5, bf16[1024,512]{1,0:T(8,128)(2,1)} %values.5), custom_call_target="tpu_custom_call" | custom-call | flops 134217728 | bytes 2097152 | tf_op jit(solution)/shard_map/states/pallas_call | solution.py:83
  2.5 19.1 %all_to_all.15.got = f32[16,32,128]{2,1,0:T(8,128)S(1)} all-to-all(f32[16,32,128]{2,1,0:T(8,128)S(1)} %bitcast.4), channel_id=1, replica_groups={{0,8,16,24,128,136,144,152,256,264,272,280,384,392,400,408},{32,40,48,5..., dimensions={0} | all-to-all | bytes 524288 | tf_op jit(solution)/shard_map/all_to_all | solution.py:162
  21.7 1.9 %collective-permute-start.1 = (f32[4,32,128]{2,1,0:T(8,128)S(1)}, f32[4,32,128]{2,1,0:T(8,128)S(1)}, u32[]{:S(2)}, u32[]{:S(2)}) collective-permute-start(f32[4,32,128]{2,1,0:T(8,128)S(1)} %get-tuple-element.22), channel_id=1, source_target_pairs={{32,0},{64,32},{40,8},{72,40},{48,16},{80,48},{56,24},{88,56},{160... | collective-permute-start | bytes 196616 | tf_op jit(solution)/shard_map/ppermute | solution.py:185
  23.6 0.7 collective-permute-start
  24.3 0.7 collective-permute-start.2
  25.0 1.3 %collective-permute-start.3 = (f32[4,32,128]{2,1,0:T(8,128)S(1)}, f32[4,32,128]{2,1,0:T(8,128)S(1)}, u32[]{:S(2)}, u32[]{:S(2)}) collective-permute-start(f32[4,32,128]{2,1,0:T(8,128)S(1)} %get-tuple-element.30), channel_id=1, source_target_pairs={{0,32},{64,96},{8,40},{72,104},{16,48},{80,112},{24,56},{88,120},{... | collective-permute-start | bytes 196616 | tf_op jit(solution)/shard_map/ppermute | solution.py:185
  26.3 8.2 %collective-permute-start.4 = (f32[4,32,128]{2,1,0:T(8,128)S(1)}, f32[4,32,128]{2,1,0:T(8,128)S(1)}, u32[]{:S(2)}, u32[]{:S(2)}) collective-permute-start(f32[4,32,128]{2,1,0:T(8,128)S(1)} %get-tuple-element.31), channel_id=1, source_target_pairs={{96,32},{32,96},{104,40},{40,104},{112,48},{48,112},{120,56},{56,1... | collective-permute-start | bytes 196616 | tf_op jit(solution)/shard_map/ppermute | solution.py:185
  34.5 2.0 %collective-permute-done.1.rest_0_.rest_1_ = f32[4,32,128]{2,1,0:T(8,128)S(1)} collective-permute-done((f32[4,32,128]{2,1,0:T(8,128)S(1)}, f32[4,32,128]{2,1,0:T(8,128)S(1)}, u32[]{:S(2)}, u32[]{:S(2)}) %collective-permute-start.1) | collective-permute-done | bytes 65568 | tf_op jit(solution)/shard_map/ppermute | solution.py:185
  36.4 1.3 %collective-permute-start.5 = (f32[4,32,128]{2,1,0:T(8,128)S(1)}, f32[4,32,128]{2,1,0:T(8,128)S(1)}, u32[]{:S(2)}, u32[]{:S(2)}) collective-permute-start(f32[4,32,128]{2,1,0:T(8,128)S(1)} %get-tuple-element.32), channel_id=1, source_target_pairs={{32,64},{40,72},{48,80},{56,88},{160,192},{168,200},{176,208},{184... | collective-permute-start | bytes 196616 | tf_op jit(solution)/shard_map/ppermute | solution.py:185
  37.8 0.0 copy-done.1
  37.8 0.0 copy-done
  37.8 0.0 copy-done.2
  37.9 0.0 collective-permute-done.rest_0_
  37.9 0.0 collective-permute-done.2.rest_2_
  37.9 0.7 collective-permute-start.6
  38.6 2.5 %local.3 = (f32[1024,512]{1,0:T(8,128)S(1)}, f32[4,128,128]{2,1,0:T(8,128)S(1)}, bf16[512,512]{1,0:T(8,128)(2,1)S(1)}) custom-call(bf16[1024,512]{1,0:T(8,128)(2,1)S(1)} %copy-done.2, bf16[1024,512]{1,0:T(8,128)(2,1)S(1)} %copy-done, bf16[1024,512]{1,0:T(8,128)(2,1)S(1)} %copy-done.1, ...), custom_call_target="tpu_custom_call", output_to_operand_aliasing={{0}: (4, {}), {1}: (5, {}), {2}: (6, {})} | custom-call | flops 1073741824 | bytes 5242880 | tf_op jit(solution)/shard_map/local/pallas_call | solution.py:234
  41.1 0.0 collective-permute-done.3.rest_3_
  41.1 1.3 %collective-permute-done.4.rest_4_ = f32[4,32,128]{2,1,0:T(8,128)S(1)} collective-permute-done((f32[4,32,128]{2,1,0:T(8,128)S(1)}, f32[4,32,128]{2,1,0:T(8,128)S(1)}, u32[]{:S(2)}, u32[]{:S(2)}) %collective-permute-start.4) | collective-permute-done | bytes 65568 | tf_op jit(solution)/shard_map/ppermute | solution.py:185
  42.4 0.0 collective-permute-done.5.rest_5_
  42.4 0.0 collective-permute-done.6.rest_6_
  42.5 14.4 %all_to_all.16 = f32[16,32,128]{2,1,0:T(8,128)S(1)} all-to-all(f32[16,32,128]{2,1,0:T(8,128)S(1)} %back.1), channel_id=1, replica_groups={{0,8,16,24,128,136,144,152,256,264,272,280,384,392,400,408},{32,40,48,5..., dimensions={0} | all-to-all | bytes 524288 | tf_op jit(solution)/shard_map/all_to_all | solution.py:195
  56.9 0.0 copy-start.3
  56.9 0.8 %mixed.1 = (f32[1024,512]{1,0:T(8,128)S(1)}, f32[8,8,128]{2,1,0:T(8,128)S(1)}) custom-call(bf16[1024,512]{1,0:T(8,128)(2,1)S(1)} %copy-done.2, bf16[512,512]{1,0:T(8,128)(2,1)S(1)} %get-tuple-element.27.top_queries, f32[1024,512]{1,0:T(8,128)S(1)} %get-tuple-element.28.local, f32[4,128,128]{2,1,0:T(8,128)S(1)} %bitcast.3, ...), custom_call_target="tpu_custom_call" | custom-call | flops 134217728 | bytes 5242880 | tf_op jit(solution)/shard_map/mixed/pallas_call | solution.py:274
  57.7 9.7 %all_to_all.17.squares = f32[8,8,128]{2,1,0:T(8,128)S(1)} all-to-all(f32[8,8,128]{2,1,0:T(8,128)S(1)} %get-tuple-element.34), channel_id=1, replica_groups=mesh['ctx'=64,'tp'=8] {'tp'}, dimensions={0} | all-to-all | bytes 65536 | tf_op jit(solution)/shard_map/all_to_all | solution.py:325
  67.4 0.0 copy-done.3
  67.4 1.2 %scored.1 = bf16[1024,512]{1,0:T(8,128)(2,1)} custom-call(f32[1024,512]{1,0:T(8,128)S(1)} %get-tuple-element.33.mixed, f32[8,8,128]{2,1,0:T(8,128)S(1)} %all_to_all.17.squares, f32[1,512]{1,0:T(1,128)S(1)} %bitcast.5), custom_call_target="tpu_custom_call" | custom-call | tf_op jit(solution)/shard_map/scored/pallas_call | solution.py:310
  (4 shorter events, 0.1 us)
Async XLA Ops:
  0.0 37.8 %copy-start.1 = (bf16[1024,512]{1,0:T(8,128)(2,1)S(1)}, bf16[1024,512]{1,0:T(8,128)(2,1)}, u32[]{:S(2)}) copy-start(bf16[1024,512]{1,0:T(8,128)(2,1)} %values.5) | copy-start | bytes 3145732
  0.0 37.8 %copy-start = (bf16[1024,512]{1,0:T(8,128)(2,1)S(1)}, bf16[1024,512]{1,0:T(8,128)(2,1)}, u32[]{:S(2)}) copy-start(bf16[1024,512]{1,0:T(8,128)(2,1)} %keys.5) | copy-start | bytes 3145732
  0.0 37.8 %copy-start.2 = (bf16[1024,512]{1,0:T(8,128)(2,1)S(1)}, bf16[1024,512]{1,0:T(8,128)(2,1)}, u32[]{:S(2)}) copy-start(bf16[1024,512]{1,0:T(8,128)(2,1)} %queries.5) | copy-start | bytes 3145732
  21.7 14.8 %collective-permute-start.1 = (f32[4,32,128]{2,1,0:T(8,128)S(1)}, f32[4,32,128]{2,1,0:T(8,128)S(1)}, u32[]{:S(2)}, u32[]{:S(2)}) collective-permute-start(f32[4,32,128]{2,1,0:T(8,128)S(1)} %get-tuple-element.22), channel_id=1, source_target_pairs={{32,0},{64,32},{40,8},{72,40},{48,16},{80,48},{56,24},{88,56},{160... | collective-permute-start | bytes 196616 | tf_op jit(solution)/shard_map/ppermute | solution.py:185
  23.6 14.2 %collective-permute-start = (f32[4,32,128]{2,1,0:T(8,128)S(1)}, f32[4,32,128]{2,1,0:T(8,128)S(1)}, u32[]{:S(2)}, u32[]{:S(2)}) collective-permute-start(f32[4,32,128]{2,1,0:T(8,128)S(1)} %get-tuple-element.21), channel_id=1, source_target_pairs={{64,0},{72,8},{80,16},{88,24},{192,128},{200,136},{208,144},{216,1... | collective-permute-start | bytes 196616 | tf_op jit(solution)/shard_map/ppermute | solution.py:185
  24.3 13.6 %collective-permute-start.2 = (f32[4,32,128]{2,1,0:T(8,128)S(1)}, f32[4,32,128]{2,1,0:T(8,128)S(1)}, u32[]{:S(2)}, u32[]{:S(2)}) collective-permute-start(f32[4,32,128]{2,1,0:T(8,128)S(1)} %get-tuple-element.23), channel_id=1, source_target_pairs={{96,0},{0,96},{104,8},{8,104},{112,16},{16,112},{120,24},{24,120},... | collective-permute-start | bytes 196616 | tf_op jit(solution)/shard_map/ppermute | solution.py:185
  25.0 16.2 %collective-permute-start.3 = (f32[4,32,128]{2,1,0:T(8,128)S(1)}, f32[4,32,128]{2,1,0:T(8,128)S(1)}, u32[]{:S(2)}, u32[]{:S(2)}) collective-permute-start(f32[4,32,128]{2,1,0:T(8,128)S(1)} %get-tuple-element.30), channel_id=1, source_target_pairs={{0,32},{64,96},{8,40},{72,104},{16,48},{80,112},{24,56},{88,120},{... | collective-permute-start | bytes 196616 | tf_op jit(solution)/shard_map/ppermute | solution.py:185
  26.3 16.2 %collective-permute-start.4 = (f32[4,32,128]{2,1,0:T(8,128)S(1)}, f32[4,32,128]{2,1,0:T(8,128)S(1)}, u32[]{:S(2)}, u32[]{:S(2)}) collective-permute-start(f32[4,32,128]{2,1,0:T(8,128)S(1)} %get-tuple-element.31), channel_id=1, source_target_pairs={{96,32},{32,96},{104,40},{40,104},{112,48},{48,112},{120,56},{56,1... | collective-permute-start | bytes 196616 | tf_op jit(solution)/shard_map/ppermute | solution.py:185
  36.4 6.0 %collective-permute-start.5 = (f32[4,32,128]{2,1,0:T(8,128)S(1)}, f32[4,32,128]{2,1,0:T(8,128)S(1)}, u32[]{:S(2)}, u32[]{:S(2)}) collective-permute-start(f32[4,32,128]{2,1,0:T(8,128)S(1)} %get-tuple-element.32), channel_id=1, source_target_pairs={{32,64},{40,72},{48,80},{56,88},{160,192},{168,200},{176,208},{184... | collective-permute-start | bytes 196616 | tf_op jit(solution)/shard_map/ppermute | solution.py:185
  37.9 4.5 %collective-permute-start.6 = (f32[4,32,128]{2,1,0:T(8,128)S(1)}, f32[4,32,128]{2,1,0:T(8,128)S(1)}, u32[]{:S(2)}, u32[]{:S(2)}) collective-permute-start(f32[4,32,128]{2,1,0:T(8,128)S(1)} %relay.1.rest_0_), channel_id=1, source_target_pairs={{96,64},{104,72},{112,80},{120,88},{224,192},{232,200},{240,208},{... | collective-permute-start | bytes 196616 | tf_op jit(solution)/shard_map/ppermute | solution.py:185
  56.9 10.5 %copy-start.3 = (f32[512]{0:T(512)S(1)}, f32[512]{0:T(512)}, u32[]{:S(2)}) copy-start(f32[512]{0:T(512)} %param.7) | copy-start | bytes 6148

commit v6 on v5

--- a/solution.py
+++ b/solution.py
@@ -98,17 +98,17 @@
 
 STEPS = (
     ((2, 0),),
-    ((1, 0), (2, 1),),
-    ((3, 0), (0, 3),),
+    ((2, 1), (3, 0),),
+    ((0, 3), (1, 0),),
     ((0, 1), (2, 3),),
-    ((3, 1), (1, 3),),
+    ((1, 3), (3, 1),),
     ((1, 2),),
     ((3, 2),),
 )
 RELAY = len(STEPS) - 1
 CARRIED = 2
-WITH = (0, 1)
-LOCAL_AFTER = 1
+WITH = (1, 0)
+LOCAL_AFTER = 0
 
 
 def relay_kernel(own, *rest):
@@ -121,13 +121,18 @@
             out[x] = own[x - 1] + carried[x] if x else carried[x]
 
 
+def rows_sent(step):
+    return XS if any(src < dst for src, dst in STEPS[step]) or step == RELAY else XS - 1
+
+
 def own_kernel(got, *outs):
     run = None
     for x in range(XS):
         for b in range(NEAR):
             run = got[x * NEAR + b] if run is None else run + got[x * NEAR + b]
         for out in outs:
-            out[x] = run
+            if x < out.shape[0]:
+                out[x] = run
 
 
 def back_kernel(meanwhile, got, *rest):
@@ -164,7 +169,7 @@
         own_kernel,
         in_specs=[VMEM],
         out_specs=[VMEM] * len(STEPS),
-        out_shape=[jax.ShapeDtypeStruct((XS, rows, HD), jnp.float32)] * len(STEPS),
+        out_shape=[jax.ShapeDtypeStruct((rows_sent(k), rows, HD), jnp.float32) for k in range(len(STEPS))],
         compiler_params=grant(OTHER_MIB),
         name="sent",
     )(got)
@@ -172,7 +177,7 @@
     for k, step in enumerate(STEPS):
         out = sent[k]
         if k == RELAY:
-            held = local(parts[LOCAL_AFTER])
+            held = local(sent[0])
             late = [parts[j] for j in (*WITH, CARRIED)] + [held[1]]
             out = pl.pallas_call(
                 relay_kernel,

time: 68.9 us -> 68 us (0.987)
  waiting for transfers between devices: 3.28 us -> 2.33 us
    ppermute x7, waiting for transfers between devices: 3.28 us -> 2.33 us  [exclusive_states(): parts.append(lax.ppermute(out, 'ctx', between(step)))]
  transfers between devices with their start and end apart: 7 -> 7, of which waited for: 2 -> 1; matrix products, arithmetic and copies ran while one was open for 0% -> 0% of each run, Pallas kernels for 4% -> 4%
where the time goes in v6:
time: 68 us; the launch traced here: 67.7 us
  blocking collectives  42.8 us (63%)
  starting transfers between devices  15.3 us (22%)
  Pallas kernels  7.09 us (10%)
  waiting for transfers between devices  2.33 us (3%)
    all_to_all x1, blocking collectives, exclusive_states(): got = lax.all_to_all(pieces, 'ctx', 0, 0, axis_index_groups=near_groups())  19.1 us
    ppermute x7, starting transfers between devices, exclusive_states(): parts.append(lax.ppermute(out, 'ctx', between(step)))  15.3 us
    all_to_all x1, blocking collectives, exclusive_states(): mine = lax.all_to_all(back, 'ctx', 0, 0, axis_index_groups=near_groups())  14 us
    all_to_all x1, blocking collectives, shards(): squares = lax.all_to_all(squares, 'tp', 0, 0)  9.72 us
    pallas_call x2, Pallas kernels, local_part(): pl.pallas_call(functools.partial(local_kernel, held is None), in_specs=[V...  2.56 us
    pallas_call x1, Pallas kernels, shard_state(): pl.pallas_call(state_kernel, in_specs=[HBM, HBM], out_specs=VMEM, out_sha...  2.47 us
    ppermute x7, waiting for transfers between devices, exclusive_states(): parts.append(lax.ppermute(out, 'ctx', between(step)))  2.33 us
  transfers between devices with their start and end apart: 7, of which 1 were waited for; matrix products, arithmetic and copies ran while one was open for 0% of the time, Pallas kernels for 4%

profile of v6, /device:TPU:128, one launch (start us, length us, event | category | flops | bytes accessed | tf_op | source)
XLA Modules:
  0.0 67.7 jit_solution(1043919470302406017)
XLA Ops:
  0.0 0.0 copy-start.1
  0.0 0.0 copy-start
  0.0 0.0 copy-start.2
  0.0 2.5 %states.1 = f32[4,128,128]{2,1,0:T(8,128)S(1)} custom-call(bf16[1024,512]{1,0:T(8,128)(2,1)} %keys.5, bf16[1024,512]{1,0:T(8,128)(2,1)} %values.5), custom_call_target="tpu_custom_call" | custom-call | flops 134217728 | bytes 2097152 | tf_op jit(solution)/shard_map/states/pallas_call | solution.py:83
  2.5 19.1 %all_to_all.15.got = f32[16,32,128]{2,1,0:T(8,128)S(1)} all-to-all(f32[16,32,128]{2,1,0:T(8,128)S(1)} %bitcast.4), channel_id=1, replica_groups={{0,8,16,24,128,136,144,152,256,264,272,280,384,392,400,408},{32,40,48,5..., dimensions={0} | all-to-all | bytes 524288 | tf_op jit(solution)/shard_map/all_to_all | solution.py:167
  21.7 1.3 %collective-permute-start = (f32[3,32,128]{2,1,0:T(8,128)S(1)}, f32[3,32,128]{2,1,0:T(8,128)S(1)}, u32[]{:S(2)}, u32[]{:S(2)}) collective-permute-start(f32[3,32,128]{2,1,0:T(8,128)S(1)} %get-tuple-element.21), channel_id=1, source_target_pairs={{64,32},{96,0},{72,40},{104,8},{80,48},{112,16},{88,56},{120,24},{... | collective-permute-start | bytes 147464 | tf_op jit(solution)/shard_map/ppermute | solution.py:190
  23.0 0.7 collective-permute-start.1
  23.6 1.3 %collective-permute-start.2 = (f32[4,32,128]{2,1,0:T(8,128)S(1)}, f32[4,32,128]{2,1,0:T(8,128)S(1)}, u32[]{:S(2)}, u32[]{:S(2)}) collective-permute-start(f32[4,32,128]{2,1,0:T(8,128)S(1)} %get-tuple-element.23), channel_id=1, source_target_pairs={{0,96},{32,0},{8,104},{40,8},{16,112},{48,16},{24,120},{56,24},{12... | collective-permute-start | bytes 196616 | tf_op jit(solution)/shard_map/ppermute | solution.py:190
  24.9 1.3 %collective-permute-start.3 = (f32[4,32,128]{2,1,0:T(8,128)S(1)}, f32[4,32,128]{2,1,0:T(8,128)S(1)}, u32[]{:S(2)}, u32[]{:S(2)}) collective-permute-start(f32[4,32,128]{2,1,0:T(8,128)S(1)} %get-tuple-element.30), channel_id=1, source_target_pairs={{0,32},{64,96},{8,40},{72,104},{16,48},{80,112},{24,56},{88,120},{... | collective-permute-start | bytes 196616 | tf_op jit(solution)/shard_map/ppermute | solution.py:190
  26.2 8.2 %collective-permute-start.4 = (f32[4,32,128]{2,1,0:T(8,128)S(1)}, f32[4,32,128]{2,1,0:T(8,128)S(1)}, u32[]{:S(2)}, u32[]{:S(2)}) collective-permute-start(f32[4,32,128]{2,1,0:T(8,128)S(1)} %get-tuple-element.31), channel_id=1, source_target_pairs={{32,96},{96,32},{40,104},{104,40},{48,112},{112,48},{56,120},{120,... | collective-permute-start | bytes 196616 | tf_op jit(solution)/shard_map/ppermute | solution.py:190
  34.5 0.0 copy-done.1
  34.5 0.0 copy-done
  34.5 0.0 copy-done.2
  34.5 0.0 collective-permute-done.rest_0_.rest_1_
  34.6 1.8 %collective-permute-start.5 = (f32[4,32,128]{2,1,0:T(8,128)S(1)}, f32[4,32,128]{2,1,0:T(8,128)S(1)}, u32[]{:S(2)}, u32[]{:S(2)}) collective-permute-start(f32[4,32,128]{2,1,0:T(8,128)S(1)} %get-tuple-element.32), channel_id=1, source_target_pairs={{32,64},{40,72},{48,80},{56,88},{160,192},{168,200},{176,208},{184... | collective-permute-start | bytes 196616 | tf_op jit(solution)/shard_map/ppermute | solution.py:190
  36.4 0.0 collective-permute-done.1.rest_1_.rest_0_
  36.4 0.0 collective-permute-done.2.rest_2_
  36.4 0.7 collective-permute-start.6
  37.1 2.5 %local.3 = (f32[1024,512]{1,0:T(8,128)S(1)}, f32[4,128,128]{2,1,0:T(8,128)S(1)}, bf16[512,512]{1,0:T(8,128)(2,1)S(1)}) custom-call(bf16[1024,512]{1,0:T(8,128)(2,1)S(1)} %copy-done.2, bf16[1024,512]{1,0:T(8,128)(2,1)S(1)} %copy-done, bf16[1024,512]{1,0:T(8,128)(2,1)S(1)} %copy-done.1, ...), custom_call_target="tpu_custom_call", output_to_operand_aliasing={{0}: (4, {}), {1}: (5, {}), {2}: (6, {})} | custom-call | flops 1073741824 | bytes 5242880 | tf_op jit(solution)/shard_map/local/pallas_call | solution.py:239
  39.7 0.0 collective-permute-done.3.rest_3_
  39.7 2.3 %collective-permute-done.4.rest_4_ = f32[4,32,128]{2,1,0:T(8,128)S(1)} collective-permute-done((f32[4,32,128]{2,1,0:T(8,128)S(1)}, f32[4,32,128]{2,1,0:T(8,128)S(1)}, u32[]{:S(2)}, u32[]{:S(2)}) %collective-permute-start.4) | collective-permute-done | bytes 65568 | tf_op jit(solution)/shard_map/ppermute | solution.py:190
  42.0 0.0 collective-permute-done.5.rest_5_
  42.0 0.0 collective-permute-done.6.rest_6_
  42.0 14.0 %all_to_all.16 = f32[16,32,128]{2,1,0:T(8,128)S(1)} all-to-all(f32[16,32,128]{2,1,0:T(8,128)S(1)} %back.1), channel_id=1, replica_groups={{0,8,16,24,128,136,144,152,256,264,272,280,384,392,400,408},{32,40,48,5..., dimensions={0} | all-to-all | bytes 524288 | tf_op jit(solution)/shard_map/all_to_all | solution.py:200
  56.0 0.0 copy-start.3
  56.0 0.8 %mixed.1 = (f32[1024,512]{1,0:T(8,128)S(1)}, f32[8,8,128]{2,1,0:T(8,128)S(1)}) custom-call(bf16[1024,512]{1,0:T(8,128)(2,1)S(1)} %copy-done.2, bf16[512,512]{1,0:T(8,128)(2,1)S(1)} %get-tuple-element.27.top_queries, f32[1024,512]{1,0:T(8,128)S(1)} %get-tuple-element.28.local, f32[4,128,128]{2,1,0:T(8,128)S(1)} %bitcast.3, ...), custom_call_target="tpu_custom_call" | custom-call | flops 134217728 | bytes 5242880 | tf_op jit(solution)/shard_map/mixed/pallas_call | solution.py:279
  56.8 9.7 %all_to_all.17.squares = f32[8,8,128]{2,1,0:T(8,128)S(1)} all-to-all(f32[8,8,128]{2,1,0:T(8,128)S(1)} %get-tuple-element.34), channel_id=1, replica_groups=mesh['ctx'=64,'tp'=8] {'tp'}, dimensions={0} | all-to-all | bytes 65536 | tf_op jit(solution)/shard_map/all_to_all | solution.py:330
  66.5 0.0 copy-done.3
  66.5 1.2 %scored.1 = bf16[1024,512]{1,0:T(8,128)(2,1)} custom-call(f32[1024,512]{1,0:T(8,128)S(1)} %get-tuple-element.33.mixed, f32[8,8,128]{2,1,0:T(8,128)S(1)} %all_to_all.17.squares, f32[1,512]{1,0:T(1,128)S(1)} %bitcast.5), custom_call_target="tpu_custom_call" | custom-call | tf_op jit(solution)/shard_map/scored/pallas_call | solution.py:315
  (4 shorter events, 0.1 us)
Async XLA Ops:
  0.0 34.5 %copy-start.1 = (bf16[1024,512]{1,0:T(8,128)(2,1)S(1)}, bf16[1024,512]{1,0:T(8,128)(2,1)}, u32[]{:S(2)}) copy-start(bf16[1024,512]{1,0:T(8,128)(2,1)} %values.5) | copy-start | bytes 3145732
  0.0 34.5 %copy-start = (bf16[1024,512]{1,0:T(8,128)(2,1)S(1)}, bf16[1024,512]{1,0:T(8,128)(2,1)}, u32[]{:S(2)}) copy-start(bf16[1024,512]{1,0:T(8,128)(2,1)} %keys.5) | copy-start | bytes 3145732
  0.0 34.5 %copy-start.2 = (bf16[1024,512]{1,0:T(8,128)(2,1)S(1)}, bf16[1024,512]{1,0:T(8,128)(2,1)}, u32[]{:S(2)}) copy-start(bf16[1024,512]{1,0:T(8,128)(2,1)} %queries.5) | copy-start | bytes 3145732
  21.7 12.9 %collective-permute-start = (f32[3,32,128]{2,1,0:T(8,128)S(1)}, f32[3,32,128]{2,1,0:T(8,128)S(1)}, u32[]{:S(2)}, u32[]{:S(2)}) collective-permute-start(f32[3,32,128]{2,1,0:T(8,128)S(1)} %get-tuple-element.21), channel_id=1, source_target_pairs={{64,32},{96,0},{72,40},{104,8},{80,48},{112,16},{88,56},{120,24},{... | collective-permute-start | bytes 147464 | tf_op jit(solution)/shard_map/ppermute | solution.py:190
  23.0 13.4 %collective-permute-start.1 = (f32[3,32,128]{2,1,0:T(8,128)S(1)}, f32[3,32,128]{2,1,0:T(8,128)S(1)}, u32[]{:S(2)}, u32[]{:S(2)}) collective-permute-start(f32[3,32,128]{2,1,0:T(8,128)S(1)} %get-tuple-element.22.rest_0_), channel_id=1, source_target_pairs={{64,0},{72,8},{80,16},{88,24},{192,128},{200,136},{208,144},{216,1... | collective-permute-start | bytes 147464 | tf_op jit(solution)/shard_map/ppermute | solution.py:190
  23.6 12.8 %collective-permute-start.2 = (f32[4,32,128]{2,1,0:T(8,128)S(1)}, f32[4,32,128]{2,1,0:T(8,128)S(1)}, u32[]{:S(2)}, u32[]{:S(2)}) collective-permute-start(f32[4,32,128]{2,1,0:T(8,128)S(1)} %get-tuple-element.23), channel_id=1, source_target_pairs={{0,96},{32,0},{8,104},{40,8},{16,112},{48,16},{24,120},{56,24},{12... | collective-permute-start | bytes 196616 | tf_op jit(solution)/shard_map/ppermute | solution.py:190
  24.9 14.7 %collective-permute-start.3 = (f32[4,32,128]{2,1,0:T(8,128)S(1)}, f32[4,32,128]{2,1,0:T(8,128)S(1)}, u32[]{:S(2)}, u32[]{:S(2)}) collective-permute-start(f32[4,32,128]{2,1,0:T(8,128)S(1)} %get-tuple-element.30), channel_id=1, source_target_pairs={{0,32},{64,96},{8,40},{72,104},{16,48},{80,112},{24,56},{88,120},{... | collective-permute-start | bytes 196616 | tf_op jit(solution)/shard_map/ppermute | solution.py:190
  26.2 15.7 %collective-permute-start.4 = (f32[4,32,128]{2,1,0:T(8,128)S(1)}, f32[4,32,128]{2,1,0:T(8,128)S(1)}, u32[]{:S(2)}, u32[]{:S(2)}) collective-permute-start(f32[4,32,128]{2,1,0:T(8,128)S(1)} %get-tuple-element.31), channel_id=1, source_target_pairs={{32,96},{96,32},{40,104},{104,40},{48,112},{112,48},{56,120},{120,... | collective-permute-start | bytes 196616 | tf_op jit(solution)/shard_map/ppermute | solution.py:190
  34.6 7.4 %collective-permute-start.5 = (f32[4,32,128]{2,1,0:T(8,128)S(1)}, f32[4,32,128]{2,1,0:T(8,128)S(1)}, u32[]{:S(2)}, u32[]{:S(2)}) collective-permute-start(f32[4,32,128]{2,1,0:T(8,128)S(1)} %get-tuple-element.32), channel_id=1, source_target_pairs={{32,64},{40,72},{48,80},{56,88},{160,192},{168,200},{176,208},{184... | collective-permute-start | bytes 196616 | tf_op jit(solution)/shard_map/ppermute | solution.py:190
  36.4 5.5 %collective-permute-start.6 = (f32[4,32,128]{2,1,0:T(8,128)S(1)}, f32[4,32,128]{2,1,0:T(8,128)S(1)}, u32[]{:S(2)}, u32[]{:S(2)}) collective-permute-start(f32[4,32,128]{2,1,0:T(8,128)S(1)} %relay.1.rest_0_), channel_id=1, source_target_pairs={{96,64},{104,72},{112,80},{120,88},{224,192},{232,200},{240,208},{... | collective-permute-start | bytes 196616 | tf_op jit(solution)/shard_map/ppermute | solution.py:190
  56.0 10.5 %copy-start.3 = (f32[512]{0:T(512)S(1)}, f32[512]{0:T(512)}, u32[]{:S(2)}) copy-start(f32[512]{0:T(512)} %param.7) | copy-start | bytes 6148

commit v7 on v6

--- a/solution.py
+++ b/solution.py
@@ -16,8 +16,8 @@
 FAR = ZS // NEAR
 MEMBERS = XS * NEAR
 PEERS = 8
-LOAD = 128
-CHUNK = 256
+LOAD = 512
+CHUNK = 512
 STORE = 128
 VMEM = pl.BlockSpec(memory_space=pltpu.VMEM)
 HBM = pl.BlockSpec(memory_space=pltpu.HBM)

time: 68 us -> 67.7 us (level)
  no operation moved by 1% of the time
where the time goes in v7:
time: 67.7 us; the launch traced here: 67.4 us
  blocking collectives  42.8 us (63%)
  starting transfers between devices  15.3 us (23%)
  Pallas kernels  6.8 us (10%)
  waiting for transfers between devices  2.34 us (3%)
    all_to_all x1, blocking collectives, exclusive_states(): got = lax.all_to_all(pieces, 'ctx', 0, 0, axis_index_groups=near_groups())  19.2 us
    ppermute x7, starting transfers between devices, exclusive_states(): parts.append(lax.ppermute(out, 'ctx', between(step)))  15.3 us
    all_to_all x1, blocking collectives, exclusive_states(): mine = lax.all_to_all(back, 'ctx', 0, 0, axis_index_groups=near_groups())  13.9 us
    all_to_all x1, blocking collectives, shards(): squares = lax.all_to_all(squares, 'tp', 0, 0)  9.72 us
    pallas_call x2, Pallas kernels, local_part(): pl.pallas_call(functools.partial(local_kernel, held is None), in_specs=[V...  2.56 us
    ppermute x7, waiting for transfers between devices, exclusive_states(): parts.append(lax.ppermute(out, 'ctx', between(step)))  2.34 us
    pallas_call x1, Pallas kernels, shard_state(): pl.pallas_call(state_kernel, in_specs=[HBM, HBM], out_specs=VMEM, out_sha...  2.18 us
  transfers between devices with their start and end apart: 7, of which 1 were waited for; matrix products, arithmetic and copies ran while one was open for 0% of the time, Pallas kernels for 4%

profile of v7, /device:TPU:128, one launch (start us, length us, event | category | flops | bytes accessed | tf_op | source)
XLA Modules:
  0.0 67.4 jit_solution(17957411877796417592)
XLA Ops:
  0.0 0.0 copy-start.1
  0.0 0.0 copy-start
  0.0 0.0 copy-start.2
  0.0 2.2 %states.1 = f32[4,128,128]{2,1,0:T(8,128)S(1)} custom-call(bf16[1024,512]{1,0:T(8,128)(2,1)} %keys.5, bf16[1024,512]{1,0:T(8,128)(2,1)} %values.5), custom_call_target="tpu_custom_call" | custom-call | flops 134217728 | bytes 2097152 | tf_op jit(solution)/shard_map/states/pallas_call | solution.py:83
  2.2 19.2 %all_to_all.15.got = f32[16,32,128]{2,1,0:T(8,128)S(1)} all-to-all(f32[16,32,128]{2,1,0:T(8,128)S(1)} %bitcast.4), channel_id=1, replica_groups={{0,8,16,24,128,136,144,152,256,264,272,280,384,392,400,408},{32,40,48,5..., dimensions={0} | all-to-all | bytes 524288 | tf_op jit(solution)/shard_map/all_to_all | solution.py:167
  21.4 1.3 %collective-permute-start = (f32[3,32,128]{2,1,0:T(8,128)S(1)}, f32[3,32,128]{2,1,0:T(8,128)S(1)}, u32[]{:S(2)}, u32[]{:S(2)}) collective-permute-start(f32[3,32,128]{2,1,0:T(8,128)S(1)} %get-tuple-element.21), channel_id=1, source_target_pairs={{64,32},{96,0},{72,40},{104,8},{80,48},{112,16},{88,56},{120,24},{... | collective-permute-start | bytes 147464 | tf_op jit(solution)/shard_map/ppermute | solution.py:190
  22.7 0.7 collective-permute-start.1
  23.4 1.3 %collective-permute-start.2 = (f32[4,32,128]{2,1,0:T(8,128)S(1)}, f32[4,32,128]{2,1,0:T(8,128)S(1)}, u32[]{:S(2)}, u32[]{:S(2)}) collective-permute-start(f32[4,32,128]{2,1,0:T(8,128)S(1)} %get-tuple-element.23), channel_id=1, source_target_pairs={{0,96},{32,0},{8,104},{40,8},{16,112},{48,16},{24,120},{56,24},{12... | collective-permute-start | bytes 196616 | tf_op jit(solution)/shard_map/ppermute | solution.py:190
  24.7 1.3 %collective-permute-start.3 = (f32[4,32,128]{2,1,0:T(8,128)S(1)}, f32[4,32,128]{2,1,0:T(8,128)S(1)}, u32[]{:S(2)}, u32[]{:S(2)}) collective-permute-start(f32[4,32,128]{2,1,0:T(8,128)S(1)} %get-tuple-element.30), channel_id=1, source_target_pairs={{0,32},{64,96},{8,40},{72,104},{16,48},{80,112},{24,56},{88,120},{... | collective-permute-start | bytes 196616 | tf_op jit(solution)/shard_map/ppermute | solution.py:190
  26.0 8.2 %collective-permute-start.4 = (f32[4,32,128]{2,1,0:T(8,128)S(1)}, f32[4,32,128]{2,1,0:T(8,128)S(1)}, u32[]{:S(2)}, u32[]{:S(2)}) collective-permute-start(f32[4,32,128]{2,1,0:T(8,128)S(1)} %get-tuple-element.31), channel_id=1, source_target_pairs={{32,96},{96,32},{40,104},{104,40},{48,112},{112,48},{56,120},{120,... | collective-permute-start | bytes 196616 | tf_op jit(solution)/shard_map/ppermute | solution.py:190
  34.2 0.0 copy-done.1
  34.2 0.0 copy-done
  34.2 0.0 copy-done.2
  34.2 0.0 collective-permute-done.rest_0_.rest_1_
  34.3 1.8 %collective-permute-start.5 = (f32[4,32,128]{2,1,0:T(8,128)S(1)}, f32[4,32,128]{2,1,0:T(8,128)S(1)}, u32[]{:S(2)}, u32[]{:S(2)}) collective-permute-start(f32[4,32,128]{2,1,0:T(8,128)S(1)} %get-tuple-element.32), channel_id=1, source_target_pairs={{32,64},{40,72},{48,80},{56,88},{160,192},{168,200},{176,208},{184... | collective-permute-start | bytes 196616 | tf_op jit(solution)/shard_map/ppermute | solution.py:190
  36.1 0.0 collective-permute-done.1.rest_1_.rest_0_
  36.1 0.0 collective-permute-done.2.rest_2_
  36.1 0.7 collective-permute-start.6
  36.8 2.5 %local.3 = (f32[1024,512]{1,0:T(8,128)S(1)}, f32[4,128,128]{2,1,0:T(8,128)S(1)}, bf16[512,512]{1,0:T(8,128)(2,1)S(1)}) custom-call(bf16[1024,512]{1,0:T(8,128)(2,1)S(1)} %copy-done.2, bf16[1024,512]{1,0:T(8,128)(2,1)S(1)} %copy-done, bf16[1024,512]{1,0:T(8,128)(2,1)S(1)} %copy-done.1, ...), custom_call_target="tpu_custom_call", output_to_operand_aliasing={{0}: (4, {}), {1}: (5, {}), {2}: (6, {})} | custom-call | flops 1073741824 | bytes 5242880 | tf_op jit(solution)/shard_map/local/pallas_call | solution.py:239
  39.4 0.0 collective-permute-done.3.rest_3_
  39.4 2.3 %collective-permute-done.4.rest_4_ = f32[4,32,128]{2,1,0:T(8,128)S(1)} collective-permute-done((f32[4,32,128]{2,1,0:T(8,128)S(1)}, f32[4,32,128]{2,1,0:T(8,128)S(1)}, u32[]{:S(2)}, u32[]{:S(2)}) %collective-permute-start.4) | collective-permute-done | bytes 65568 | tf_op jit(solution)/shard_map/ppermute | solution.py:190
  41.7 0.0 collective-permute-done.5.rest_5_
  41.7 0.0 collective-permute-done.6.rest_6_
  41.8 13.9 %all_to_all.16 = f32[16,32,128]{2,1,0:T(8,128)S(1)} all-to-all(f32[16,32,128]{2,1,0:T(8,128)S(1)} %back.1), channel_id=1, replica_groups={{0,8,16,24,128,136,144,152,256,264,272,280,384,392,400,408},{32,40,48,5..., dimensions={0} | all-to-all | bytes 524288 | tf_op jit(solution)/shard_map/all_to_all | solution.py:200
  55.7 0.0 copy-start.3
  55.7 0.8 %mixed.1 = (f32[1024,512]{1,0:T(8,128)S(1)}, f32[8,8,128]{2,1,0:T(8,128)S(1)}) custom-call(bf16[1024,512]{1,0:T(8,128)(2,1)S(1)} %copy-done.2, bf16[512,512]{1,0:T(8,128)(2,1)S(1)} %get-tuple-element.27.top_queries, f32[1024,512]{1,0:T(8,128)S(1)} %get-tuple-element.28.local, f32[4,128,128]{2,1,0:T(8,128)S(1)} %bitcast.3, ...), custom_call_target="tpu_custom_call" | custom-call | flops 134217728 | bytes 5242880 | tf_op jit(solution)/shard_map/mixed/pallas_call | solution.py:279
  56.5 9.7 %all_to_all.17.squares = f32[8,8,128]{2,1,0:T(8,128)S(1)} all-to-all(f32[8,8,128]{2,1,0:T(8,128)S(1)} %get-tuple-element.34), channel_id=1, replica_groups=mesh['ctx'=64,'tp'=8] {'tp'}, dimensions={0} | all-to-all | bytes 65536 | tf_op jit(solution)/shard_map/all_to_all | solution.py:330
  66.2 0.0 copy-done.3
  66.2 1.2 %scored.1 = bf16[1024,512]{1,0:T(8,128)(2,1)} custom-call(f32[1024,512]{1,0:T(8,128)S(1)} %get-tuple-element.33.mixed, f32[8,8,128]{2,1,0:T(8,128)S(1)} %all_to_all.17.squares, f32[1,512]{1,0:T(1,128)S(1)} %bitcast.5), custom_call_target="tpu_custom_call" | custom-call | tf_op jit(solution)/shard_map/scored/pallas_call | solution.py:315
  (4 shorter events, 0.1 us)
Async XLA Ops:
  0.0 34.2 %copy-start.1 = (bf16[1024,512]{1,0:T(8,128)(2,1)S(1)}, bf16[1024,512]{1,0:T(8,128)(2,1)}, u32[]{:S(2)}) copy-start(bf16[1024,512]{1,0:T(8,128)(2,1)} %values.5) | copy-start | bytes 3145732
  0.0 34.2 %copy-start = (bf16[1024,512]{1,0:T(8,128)(2,1)S(1)}, bf16[1024,512]{1,0:T(8,128)(2,1)}, u32[]{:S(2)}) copy-start(bf16[1024,512]{1,0:T(8,128)(2,1)} %keys.5) | copy-start | bytes 3145732
  0.0 34.2 %copy-start.2 = (bf16[1024,512]{1,0:T(8,128)(2,1)S(1)}, bf16[1024,512]{1,0:T(8,128)(2,1)}, u32[]{:S(2)}) copy-start(bf16[1024,512]{1,0:T(8,128)(2,1)} %queries.5) | copy-start | bytes 3145732
  21.4 12.9 %collective-permute-start = (f32[3,32,128]{2,1,0:T(8,128)S(1)}, f32[3,32,128]{2,1,0:T(8,128)S(1)}, u32[]{:S(2)}, u32[]{:S(2)}) collective-permute-start(f32[3,32,128]{2,1,0:T(8,128)S(1)} %get-tuple-element.21), channel_id=1, source_target_pairs={{64,32},{96,0},{72,40},{104,8},{80,48},{112,16},{88,56},{120,24},{... | collective-permute-start | bytes 147464 | tf_op jit(solution)/shard_map/ppermute | solution.py:190
  22.7 13.4 %collective-permute-start.1 = (f32[3,32,128]{2,1,0:T(8,128)S(1)}, f32[3,32,128]{2,1,0:T(8,128)S(1)}, u32[]{:S(2)}, u32[]{:S(2)}) collective-permute-start(f32[3,32,128]{2,1,0:T(8,128)S(1)} %get-tuple-element.22.rest_0_), channel_id=1, source_target_pairs={{64,0},{72,8},{80,16},{88,24},{192,128},{200,136},{208,144},{216,1... | collective-permute-start | bytes 147464 | tf_op jit(solution)/shard_map/ppermute | solution.py:190
  23.4 12.8 %collective-permute-start.2 = (f32[4,32,128]{2,1,0:T(8,128)S(1)}, f32[4,32,128]{2,1,0:T(8,128)S(1)}, u32[]{:S(2)}, u32[]{:S(2)}) collective-permute-start(f32[4,32,128]{2,1,0:T(8,128)S(1)} %get-tuple-element.23), channel_id=1, source_target_pairs={{0,96},{32,0},{8,104},{40,8},{16,112},{48,16},{24,120},{56,24},{12... | collective-permute-start | bytes 196616 | tf_op jit(solution)/shard_map/ppermute | solution.py:190
  24.7 14.7 %collective-permute-start.3 = (f32[4,32,128]{2,1,0:T(8,128)S(1)}, f32[4,32,128]{2,1,0:T(8,128)S(1)}, u32[]{:S(2)}, u32[]{:S(2)}) collective-permute-start(f32[4,32,128]{2,1,0:T(8,128)S(1)} %get-tuple-element.30), channel_id=1, source_target_pairs={{0,32},{64,96},{8,40},{72,104},{16,48},{80,112},{24,56},{88,120},{... | collective-permute-start | bytes 196616 | tf_op jit(solution)/shard_map/ppermute | solution.py:190
  26.0 15.7 %collective-permute-start.4 = (f32[4,32,128]{2,1,0:T(8,128)S(1)}, f32[4,32,128]{2,1,0:T(8,128)S(1)}, u32[]{:S(2)}, u32[]{:S(2)}) collective-permute-start(f32[4,32,128]{2,1,0:T(8,128)S(1)} %get-tuple-element.31), channel_id=1, source_target_pairs={{32,96},{96,32},{40,104},{104,40},{48,112},{112,48},{56,120},{120,... | collective-permute-start | bytes 196616 | tf_op jit(solution)/shard_map/ppermute | solution.py:190
  34.3 7.4 %collective-permute-start.5 = (f32[4,32,128]{2,1,0:T(8,128)S(1)}, f32[4,32,128]{2,1,0:T(8,128)S(1)}, u32[]{:S(2)}, u32[]{:S(2)}) collective-permute-start(f32[4,32,128]{2,1,0:T(8,128)S(1)} %get-tuple-element.32), channel_id=1, source_target_pairs={{32,64},{40,72},{48,80},{56,88},{160,192},{168,200},{176,208},{184... | collective-permute-start | bytes 196616 | tf_op jit(solution)/shard_map/ppermute | solution.py:190
  36.1 5.5 %collective-permute-start.6 = (f32[4,32,128]{2,1,0:T(8,128)S(1)}, f32[4,32,128]{2,1,0:T(8,128)S(1)}, u32[]{:S(2)}, u32[]{:S(2)}) collective-permute-start(f32[4,32,128]{2,1,0:T(8,128)S(1)} %relay.1.rest_0_), channel_id=1, source_target_pairs={{96,64},{104,72},{112,80},{120,88},{224,192},{232,200},{240,208},{... | collective-permute-start | bytes 196616 | tf_op jit(solution)/shard_map/ppermute | solution.py:190
  55.7 10.5 %copy-start.3 = (f32[512]{0:T(512)S(1)}, f32[512]{0:T(512)}, u32[]{:S(2)}) copy-start(f32[512]{0:T(512)} %param.7) | copy-start | bytes 6148

commit v8 on v7

--- a/solution.py
+++ b/solution.py
@@ -98,8 +98,8 @@
 
 STEPS = (
     ((2, 0),),
-    ((2, 1), (3, 0),),
-    ((0, 3), (1, 0),),
+    ((3, 0),),
+    ((0, 3), (1, 0), (2, 1),),
     ((0, 1), (2, 3),),
     ((1, 3), (3, 1),),
     ((1, 2),),

time: 67.7 us -> 67.9 us (level)
  blocking collectives: 42.8 us -> 43.7 us
  waiting for transfers between devices: 2.34 us -> 1.66 us
    all_to_all x1, blocking collectives: 13.9 us -> 14.8 us  [exclusive_states(): mine = lax.all_to_all(back, 'ctx', 0, 0, axis_index_groups=near_groups())]
    ppermute x7, waiting for transfers between devices: 2.34 us -> 1.66 us  [exclusive_states(): parts.append(lax.ppermute(out, 'ctx', between(step)))]
where the time goes in v8:
time: 67.9 us; the launch traced here: 67.6 us
  blocking collectives  43.7 us (64%)
  starting transfers between devices  15.3 us (23%)
  Pallas kernels  6.8 us (10%)
  waiting for transfers between devices  1.66 us (2%)
    all_to_all x1, blocking collectives, exclusive_states(): got = lax.all_to_all(pieces, 'ctx', 0, 0, axis_index_groups=near_groups())  19.2 us
    ppermute x7, starting transfers between devices, exclusive_states(): parts.append(lax.ppermute(out, 'ctx', between(step)))  15.3 us
    all_to_all x1, blocking collectives, exclusive_states(): mine = lax.all_to_all(back, 'ctx', 0, 0, axis_index_groups=near_groups())  14.8 us
    all_to_all x1, blocking collectives, shards(): squares = lax.all_to_all(squares, 'tp', 0, 0)  9.72 us
    pallas_call x2, Pallas kernels, local_part(): pl.pallas_call(functools.partial(local_kernel, held is None), in_specs=[V...  2.56 us
    pallas_call x1, Pallas kernels, shard_state(): pl.pallas_call(state_kernel, in_specs=[HBM, HBM], out_specs=VMEM, out_sha...  2.18 us
    ppermute x7, waiting for transfers between devices, exclusive_states(): parts.append(lax.ppermute(out, 'ctx', between(step)))  1.66 us
  transfers between devices with their start and end apart: 7, of which 1 were waited for; matrix products, arithmetic and copies ran while one was open for 0% of the time, Pallas kernels for 4%

profile of v8, /device:TPU:128, one launch (start us, length us, event | category | flops | bytes accessed | tf_op | source)
XLA Modules:
  0.0 67.6 jit_solution(13878339256400433048)
XLA Ops:
  0.0 0.0 copy-start.1
  0.0 0.0 copy-start
  0.0 0.0 copy-start.2
  0.0 2.2 %states.1 = f32[4,128,128]{2,1,0:T(8,128)S(1)} custom-call(bf16[1024,512]{1,0:T(8,128)(2,1)} %keys.5, bf16[1024,512]{1,0:T(8,128)(2,1)} %values.5), custom_call_target="tpu_custom_call" | custom-call | flops 134217728 | bytes 2097152 | tf_op jit(solution)/shard_map/states/pallas_call | solution.py:83
  2.2 19.2 %all_to_all.15.got = f32[16,32,128]{2,1,0:T(8,128)S(1)} all-to-all(f32[16,32,128]{2,1,0:T(8,128)S(1)} %bitcast.4), channel_id=1, replica_groups={{0,8,16,24,128,136,144,152,256,264,272,280,384,392,400,408},{32,40,48,5..., dimensions={0} | all-to-all | bytes 524288 | tf_op jit(solution)/shard_map/all_to_all | solution.py:167
  21.4 0.7 collective-permute-start
  22.1 0.7 collective-permute-start.1
  22.7 1.9 %collective-permute-start.2 = (f32[4,32,128]{2,1,0:T(8,128)S(1)}, f32[4,32,128]{2,1,0:T(8,128)S(1)}, u32[]{:S(2)}, u32[]{:S(2)}) collective-permute-start(f32[4,32,128]{2,1,0:T(8,128)S(1)} %get-tuple-element.23), channel_id=1, source_target_pairs={{0,96},{32,0},{64,32},{8,104},{40,8},{72,40},{16,112},{48,16},{80,... | collective-permute-start | bytes 196616 | tf_op jit(solution)/shard_map/ppermute | solution.py:190
  24.7 1.3 %collective-permute-start.3 = (f32[4,32,128]{2,1,0:T(8,128)S(1)}, f32[4,32,128]{2,1,0:T(8,128)S(1)}, u32[]{:S(2)}, u32[]{:S(2)}) collective-permute-start(f32[4,32,128]{2,1,0:T(8,128)S(1)} %get-tuple-element.30), channel_id=1, source_target_pairs={{0,32},{64,96},{8,40},{72,104},{16,48},{80,112},{24,56},{88,120},{... | collective-permute-start | bytes 196616 | tf_op jit(solution)/shard_map/ppermute | solution.py:190
  26.0 8.2 %collective-permute-start.4 = (f32[4,32,128]{2,1,0:T(8,128)S(1)}, f32[4,32,128]{2,1,0:T(8,128)S(1)}, u32[]{:S(2)}, u32[]{:S(2)}) collective-permute-start(f32[4,32,128]{2,1,0:T(8,128)S(1)} %get-tuple-element.31), channel_id=1, source_target_pairs={{32,96},{96,32},{40,104},{104,40},{48,112},{112,48},{56,120},{120,... | collective-permute-start | bytes 196616 | tf_op jit(solution)/shard_map/ppermute | solution.py:190
  34.2 0.0 copy-done.1
  34.2 0.0 copy-done
  34.2 0.0 copy-done.2
  34.2 0.0 collective-permute-done.rest_0_.rest_1_
  34.3 1.8 %collective-permute-start.5 = (f32[4,32,128]{2,1,0:T(8,128)S(1)}, f32[4,32,128]{2,1,0:T(8,128)S(1)}, u32[]{:S(2)}, u32[]{:S(2)}) collective-permute-start(f32[4,32,128]{2,1,0:T(8,128)S(1)} %get-tuple-element.32), channel_id=1, source_target_pairs={{32,64},{40,72},{48,80},{56,88},{160,192},{168,200},{176,208},{184... | collective-permute-start | bytes 196616 | tf_op jit(solution)/shard_map/ppermute | solution.py:190
  36.1 0.0 collective-permute-done.1.rest_1_.rest_0_
  36.1 0.0 collective-permute-done.2.rest_2_
  36.1 0.7 collective-permute-start.6
  36.8 2.5 %local.3 = (f32[1024,512]{1,0:T(8,128)S(1)}, f32[4,128,128]{2,1,0:T(8,128)S(1)}, bf16[512,512]{1,0:T(8,128)(2,1)S(1)}) custom-call(bf16[1024,512]{1,0:T(8,128)(2,1)S(1)} %copy-done.2, bf16[1024,512]{1,0:T(8,128)(2,1)S(1)} %copy-done, bf16[1024,512]{1,0:T(8,128)(2,1)S(1)} %copy-done.1, ...), custom_call_target="tpu_custom_call", output_to_operand_aliasing={{0}: (4, {}), {1}: (5, {}), {2}: (6, {})} | custom-call | flops 1073741824 | bytes 5242880 | tf_op jit(solution)/shard_map/local/pallas_call | solution.py:239
  39.4 0.0 collective-permute-done.3.rest_3_
  39.4 1.6 %collective-permute-done.4.rest_4_ = f32[4,32,128]{2,1,0:T(8,128)S(1)} collective-permute-done((f32[4,32,128]{2,1,0:T(8,128)S(1)}, f32[4,32,128]{2,1,0:T(8,128)S(1)}, u32[]{:S(2)}, u32[]{:S(2)}) %collective-permute-start.4) | collective-permute-done | bytes 65568 | tf_op jit(solution)/shard_map/ppermute | solution.py:190
  41.0 0.0 collective-permute-done.5.rest_5_
  41.0 0.0 collective-permute-done.6.rest_6_
  41.1 14.8 %all_to_all.16 = f32[16,32,128]{2,1,0:T(8,128)S(1)} all-to-all(f32[16,32,128]{2,1,0:T(8,128)S(1)} %back.1), channel_id=1, replica_groups={{0,8,16,24,128,136,144,152,256,264,272,280,384,392,400,408},{32,40,48,5..., dimensions={0} | all-to-all | bytes 524288 | tf_op jit(solution)/shard_map/all_to_all | solution.py:200
  55.9 0.0 copy-start.3
  55.9 0.8 %mixed.1 = (f32[1024,512]{1,0:T(8,128)S(1)}, f32[8,8,128]{2,1,0:T(8,128)S(1)}) custom-call(bf16[1024,512]{1,0:T(8,128)(2,1)S(1)} %copy-done.2, bf16[512,512]{1,0:T(8,128)(2,1)S(1)} %get-tuple-element.27.top_queries, f32[1024,512]{1,0:T(8,128)S(1)} %get-tuple-element.28.local, f32[4,128,128]{2,1,0:T(8,128)S(1)} %bitcast.3, ...), custom_call_target="tpu_custom_call" | custom-call | flops 134217728 | bytes 5242880 | tf_op jit(solution)/shard_map/mixed/pallas_call | solution.py:279
  56.7 9.7 %all_to_all.17.squares = f32[8,8,128]{2,1,0:T(8,128)S(1)} all-to-all(f32[8,8,128]{2,1,0:T(8,128)S(1)} %get-tuple-element.34), channel_id=1, replica_groups=mesh['ctx'=64,'tp'=8] {'tp'}, dimensions={0} | all-to-all | bytes 65536 | tf_op jit(solution)/shard_map/all_to_all | solution.py:330
  66.5 0.0 copy-done.3
  66.5 1.2 %scored.1 = bf16[1024,512]{1,0:T(8,128)(2,1)} custom-call(f32[1024,512]{1,0:T(8,128)S(1)} %get-tuple-element.33.mixed, f32[8,8,128]{2,1,0:T(8,128)S(1)} %all_to_all.17.squares, f32[1,512]{1,0:T(1,128)S(1)} %bitcast.5), custom_call_target="tpu_custom_call" | custom-call | tf_op jit(solution)/shard_map/scored/pallas_call | solution.py:315
  (4 shorter events, 0.1 us)
Async XLA Ops:
  0.0 34.2 %copy-start.1 = (bf16[1024,512]{1,0:T(8,128)(2,1)S(1)}, bf16[1024,512]{1,0:T(8,128)(2,1)}, u32[]{:S(2)}) copy-start(bf16[1024,512]{1,0:T(8,128)(2,1)} %values.5) | copy-start | bytes 3145732
  0.0 34.2 %copy-start = (bf16[1024,512]{1,0:T(8,128)(2,1)S(1)}, bf16[1024,512]{1,0:T(8,128)(2,1)}, u32[]{:S(2)}) copy-start(bf16[1024,512]{1,0:T(8,128)(2,1)} %keys.5) | copy-start | bytes 3145732
  0.0 34.2 %copy-start.2 = (bf16[1024,512]{1,0:T(8,128)(2,1)S(1)}, bf16[1024,512]{1,0:T(8,128)(2,1)}, u32[]{:S(2)}) copy-start(bf16[1024,512]{1,0:T(8,128)(2,1)} %queries.5) | copy-start | bytes 3145732
  21.4 12.9 %collective-permute-start = (f32[3,32,128]{2,1,0:T(8,128)S(1)}, f32[3,32,128]{2,1,0:T(8,128)S(1)}, u32[]{:S(2)}, u32[]{:S(2)}) collective-permute-start(f32[3,32,128]{2,1,0:T(8,128)S(1)} %get-tuple-element.21), channel_id=1, source_target_pairs={{96,0},{104,8},{112,16},{120,24},{224,128},{232,136},{240,144},{24... | collective-permute-start | bytes 147464 | tf_op jit(solution)/shard_map/ppermute | solution.py:190
  22.1 14.1 %collective-permute-start.1 = (f32[3,32,128]{2,1,0:T(8,128)S(1)}, f32[3,32,128]{2,1,0:T(8,128)S(1)}, u32[]{:S(2)}, u32[]{:S(2)}) collective-permute-start(f32[3,32,128]{2,1,0:T(8,128)S(1)} %get-tuple-element.22.rest_0_), channel_id=1, source_target_pairs={{64,0},{72,8},{80,16},{88,24},{192,128},{200,136},{208,144},{216,1... | collective-permute-start | bytes 147464 | tf_op jit(solution)/shard_map/ppermute | solution.py:190
  22.7 13.4 %collective-permute-start.2 = (f32[4,32,128]{2,1,0:T(8,128)S(1)}, f32[4,32,128]{2,1,0:T(8,128)S(1)}, u32[]{:S(2)}, u32[]{:S(2)}) collective-permute-start(f32[4,32,128]{2,1,0:T(8,128)S(1)} %get-tuple-element.23), channel_id=1, source_target_pairs={{0,96},{32,0},{64,32},{8,104},{40,8},{72,40},{16,112},{48,16},{80,... | collective-permute-start | bytes 196616 | tf_op jit(solution)/shard_map/ppermute | solution.py:190
  24.7 14.7 %collective-permute-start.3 = (f32[4,32,128]{2,1,0:T(8,128)S(1)}, f32[4,32,128]{2,1,0:T(8,128)S(1)}, u32[]{:S(2)}, u32[]{:S(2)}) collective-permute-start(f32[4,32,128]{2,1,0:T(8,128)S(1)} %get-tuple-element.30), channel_id=1, source_target_pairs={{0,32},{64,96},{8,40},{72,104},{16,48},{80,112},{24,56},{88,120},{... | collective-permute-start | bytes 196616 | tf_op jit(solution)/shard_map/ppermute | solution.py:190
  26.0 15.1 %collective-permute-start.4 = (f32[4,32,128]{2,1,0:T(8,128)S(1)}, f32[4,32,128]{2,1,0:T(8,128)S(1)}, u32[]{:S(2)}, u32[]{:S(2)}) collective-permute-start(f32[4,32,128]{2,1,0:T(8,128)S(1)} %get-tuple-element.31), channel_id=1, source_target_pairs={{32,96},{96,32},{40,104},{104,40},{48,112},{112,48},{56,120},{120,... | collective-permute-start | bytes 196616 | tf_op jit(solution)/shard_map/ppermute | solution.py:190
  34.3 6.8 %collective-permute-start.5 = (f32[4,32,128]{2,1,0:T(8,128)S(1)}, f32[4,32,128]{2,1,0:T(8,128)S(1)}, u32[]{:S(2)}, u32[]{:S(2)}) collective-permute-start(f32[4,32,128]{2,1,0:T(8,128)S(1)} %get-tuple-element.32), channel_id=1, source_target_pairs={{32,64},{40,72},{48,80},{56,88},{160,192},{168,200},{176,208},{184... | collective-permute-start | bytes 196616 | tf_op jit(solution)/shard_map/ppermute | solution.py:190
  36.1 4.9 %collective-permute-start.6 = (f32[4,32,128]{2,1,0:T(8,128)S(1)}, f32[4,32,128]{2,1,0:T(8,128)S(1)}, u32[]{:S(2)}, u32[]{:S(2)}) collective-permute-start(f32[4,32,128]{2,1,0:T(8,128)S(1)} %relay.1.rest_0_), channel_id=1, source_target_pairs={{96,64},{104,72},{112,80},{120,88},{224,192},{232,200},{240,208},{... | collective-permute-start | bytes 196616 | tf_op jit(solution)/shard_map/ppermute | solution.py:190
  55.9 10.5 %copy-start.3 = (f32[512]{0:T(512)S(1)}, f32[512]{0:T(512)}, u32[]{:S(2)}) copy-start(f32[512]{0:T(512)} %param.7) | copy-start | bytes 6148

commit v9 on v7

--- a/solution.py
+++ b/solution.py
@@ -10,6 +10,7 @@
 HD = 128
 D = 4096
 BLOCK = 512
+KEPT = 640
 XS = 4
 ZS = 16
 NEAR = 4
@@ -215,7 +216,7 @@
     row = lax.broadcasted_iota(jnp.int32, (half, half), 0)
     col = lax.broadcasted_iota(jnp.int32, (half, half), 1)
     lower = row >= col
-    top_queries[...] = queries[:BLOCK]
+    top_queries[...] = queries[:KEPT]
     for h in range(queries.shape[1] // HD):
         cols = head_columns(h)
         first[h] = contract_tokens(keys[:BLOCK, cols], values[:BLOCK, cols])
@@ -243,7 +244,7 @@
         out_shape=[
             jax.ShapeDtypeStruct((rows, width), jnp.float32),
             jax.ShapeDtypeStruct((width // HD, HD, HD), jnp.float32),
-            jax.ShapeDtypeStruct((BLOCK, width), queries.dtype),
+            jax.ShapeDtypeStruct((KEPT, width), queries.dtype),
         ],
         input_output_aliases={4 + i: i for i in range(3)} if held else {},
         compiler_params=grant(LOCAL_MIB),
@@ -253,25 +254,26 @@
 
 
 def mixed_kernel(queries, top_queries, local, prefix, first, mixed, squares, held, sem):
-    tiles = BLOCK // HD
-    rest = pltpu.make_async_copy(queries.at[pl.ds(BLOCK, BLOCK)], held, sem)
+    rows = local.shape[0]
+    rest = pltpu.make_async_copy(queries.at[pl.ds(KEPT, rows - KEPT)], held, sem)
     rest.start()
-    for i in range(local.shape[0] // BLOCK):
-        if i:
+    for low_row, high_row in ((0, BLOCK), (BLOCK, KEPT), (KEPT, rows)):
+        if low_row == KEPT:
             rest.wait()
-        rows = slice(i * BLOCK, (i + 1) * BLOCK)
+        part = slice(low_row, high_row)
+        tiles = (high_row - low_row) // HD
         acc = None
         for h in range(local.shape[1] // HD):
             cols = head_columns(h)
-            state = prefix[h] + first[h] if i else prefix[h]
-            q = held[:, cols] if i else top_queries[:, cols]
-            m = jnp.dot(q, state.astype(jnp.bfloat16), preferred_element_type=jnp.float32) + local[rows, cols]
-            mixed[rows, cols] = m
+            state = prefix[h] + first[h] if low_row else prefix[h]
+            q = held[:, cols] if low_row == KEPT else top_queries[part, cols]
+            m = jnp.dot(q, state.astype(jnp.bfloat16), preferred_element_type=jnp.float32) + local[part, cols]
+            mixed[part, cols] = m
             acc = m * m if h == 0 else acc + m * m
         turned = jnp.swapaxes(acc.reshape(tiles, HD, HD), 1, 2)
         sums = jnp.sum(turned, axis=1)
         for p in range(PEERS):
-            squares[p, i * tiles : (i + 1) * tiles] = sums
+            squares[p, low_row // HD : high_row // HD] = sums
 
 
 def mixed_part(queries, top_queries, local, prefix, first):
@@ -284,7 +286,7 @@
             jax.ShapeDtypeStruct((rows, width), jnp.float32),
             jax.ShapeDtypeStruct((PEERS, rows // HD, HD), jnp.float32),
         ],
-        scratch_shapes=[pltpu.VMEM((BLOCK, width), queries.dtype), pltpu.SemaphoreType.DMA(())],
+        scratch_shapes=[pltpu.VMEM((rows - KEPT, width), queries.dtype), pltpu.SemaphoreType.DMA(())],
         compiler_params=grant(MIXED_MIB),
         cost_estimate=pl.CostEstimate(flops=2 * rows * HD * width, bytes_accessed=10 * rows * width, transcendentals=0),
         name="mixed",

time: 67.7 us -> 67.9 us (level)
  no operation moved by 1% of the time
where the time goes in v9:
time: 67.9 us; the launch traced here: 67.5 us
  blocking collectives  42.8 us (63%)
  starting transfers between devices  15.3 us (23%)
  Pallas kernels  6.97 us (10%)
  waiting for transfers between devices  2.32 us (3%)
    all_to_all x1, blocking collectives, exclusive_states(): got = lax.all_to_all(pieces, 'ctx', 0, 0, axis_index_groups=near_groups())  19.2 us
    ppermute x7, starting transfers between devices, exclusive_states(): parts.append(lax.ppermute(out, 'ctx', between(step)))  15.3 us
    all_to_all x1, blocking collectives, exclusive_states(): mine = lax.all_to_all(back, 'ctx', 0, 0, axis_index_groups=near_groups())  13.9 us
    all_to_all x1, blocking collectives, shards(): squares = lax.all_to_all(squares, 'tp', 0, 0)  9.72 us
    pallas_call x2, Pallas kernels, local_part(): pl.pallas_call(functools.partial(local_kernel, held is None), in_specs=[V...  2.58 us
    ppermute x7, waiting for transfers between devices, exclusive_states(): parts.append(lax.ppermute(out, 'ctx', between(step)))  2.32 us
    pallas_call x1, Pallas kernels, shard_state(): pl.pallas_call(state_kernel, in_specs=[HBM, HBM], out_specs=VMEM, out_sha...  2.18 us
  transfers between devices with their start and end apart: 7, of which 1 were waited for; matrix products, arithmetic and copies ran while one was open for 0% of the time, Pallas kernels for 4%

profile of v9, /device:TPU:128, one launch (start us, length us, event | category | flops | bytes accessed | tf_op | source)
XLA Modules:
  0.0 67.5 jit_solution(17425935014437823121)
XLA Ops:
  0.0 0.0 copy-start.1
  0.0 0.0 copy-start
  0.0 0.0 copy-start.2
  0.0 2.2 %states.1 = f32[4,128,128]{2,1,0:T(8,128)S(1)} custom-call(bf16[1024,512]{1,0:T(8,128)(2,1)} %keys.5, bf16[1024,512]{1,0:T(8,128)(2,1)} %values.5), custom_call_target="tpu_custom_call" | custom-call | flops 134217728 | bytes 2097152 | tf_op jit(solution)/shard_map/states/pallas_call | solution.py:84
  2.2 19.2 %all_to_all.15.got = f32[16,32,128]{2,1,0:T(8,128)S(1)} all-to-all(f32[16,32,128]{2,1,0:T(8,128)S(1)} %bitcast.4), channel_id=1, replica_groups={{0,8,16,24,128,136,144,152,256,264,272,280,384,392,400,408},{32,40,48,5..., dimensions={0} | all-to-all | bytes 524288 | tf_op jit(solution)/shard_map/all_to_all | solution.py:168
  21.4 1.3 %collective-permute-start = (f32[3,32,128]{2,1,0:T(8,128)S(1)}, f32[3,32,128]{2,1,0:T(8,128)S(1)}, u32[]{:S(2)}, u32[]{:S(2)}) collective-permute-start(f32[3,32,128]{2,1,0:T(8,128)S(1)} %get-tuple-element.21), channel_id=1, source_target_pairs={{64,32},{96,0},{72,40},{104,8},{80,48},{112,16},{88,56},{120,24},{... | collective-permute-start | bytes 147464 | tf_op jit(solution)/shard_map/ppermute | solution.py:191
  22.7 0.7 collective-permute-start.1
  23.4 1.3 %collective-permute-start.2 = (f32[4,32,128]{2,1,0:T(8,128)S(1)}, f32[4,32,128]{2,1,0:T(8,128)S(1)}, u32[]{:S(2)}, u32[]{:S(2)}) collective-permute-start(f32[4,32,128]{2,1,0:T(8,128)S(1)} %get-tuple-element.23), channel_id=1, source_target_pairs={{0,96},{32,0},{8,104},{40,8},{16,112},{48,16},{24,120},{56,24},{12... | collective-permute-start | bytes 196616 | tf_op jit(solution)/shard_map/ppermute | solution.py:191
  24.7 1.3 %collective-permute-start.3 = (f32[4,32,128]{2,1,0:T(8,128)S(1)}, f32[4,32,128]{2,1,0:T(8,128)S(1)}, u32[]{:S(2)}, u32[]{:S(2)}) collective-permute-start(f32[4,32,128]{2,1,0:T(8,128)S(1)} %get-tuple-element.30), channel_id=1, source_target_pairs={{0,32},{64,96},{8,40},{72,104},{16,48},{80,112},{24,56},{88,120},{... | collective-permute-start | bytes 196616 | tf_op jit(solution)/shard_map/ppermute | solution.py:191
  26.0 8.2 %collective-permute-start.4 = (f32[4,32,128]{2,1,0:T(8,128)S(1)}, f32[4,32,128]{2,1,0:T(8,128)S(1)}, u32[]{:S(2)}, u32[]{:S(2)}) collective-permute-start(f32[4,32,128]{2,1,0:T(8,128)S(1)} %get-tuple-element.31), channel_id=1, source_target_pairs={{32,96},{96,32},{40,104},{104,40},{48,112},{112,48},{56,120},{120,... | collective-permute-start | bytes 196616 | tf_op jit(solution)/shard_map/ppermute | solution.py:191
  34.2 0.0 copy-done.1
  34.2 0.0 copy-done
  34.2 0.0 copy-done.2
  34.2 0.0 collective-permute-done.rest_0_.rest_1_
  34.3 1.8 %collective-permute-start.5 = (f32[4,32,128]{2,1,0:T(8,128)S(1)}, f32[4,32,128]{2,1,0:T(8,128)S(1)}, u32[]{:S(2)}, u32[]{:S(2)}) collective-permute-start(f32[4,32,128]{2,1,0:T(8,128)S(1)} %get-tuple-element.32), channel_id=1, source_target_pairs={{32,64},{40,72},{48,80},{56,88},{160,192},{168,200},{176,208},{184... | collective-permute-start | bytes 196616 | tf_op jit(solution)/shard_map/ppermute | solution.py:191
  36.1 0.0 collective-permute-done.1.rest_1_.rest_0_
  36.1 0.0 collective-permute-done.2.rest_2_
  36.1 0.7 collective-permute-start.6
  36.8 2.5 %local.3 = (f32[1024,512]{1,0:T(8,128)S(1)}, f32[4,128,128]{2,1,0:T(8,128)S(1)}, bf16[640,512]{1,0:T(8,128)(2,1)S(1)}) custom-call(bf16[1024,512]{1,0:T(8,128)(2,1)S(1)} %copy-done.2, bf16[1024,512]{1,0:T(8,128)(2,1)S(1)} %copy-done, bf16[1024,512]{1,0:T(8,128)(2,1)S(1)} %copy-done.1, ...), custom_call_target="tpu_custom_call", output_to_operand_aliasing={{0}: (4, {}), {1}: (5, {}), {2}: (6, {})} | custom-call | flops 1073741824 | bytes 5242880 | tf_op jit(solution)/shard_map/local/pallas_call | solution.py:240
  39.4 0.0 collective-permute-done.3.rest_3_
  39.4 2.3 %collective-permute-done.4.rest_4_ = f32[4,32,128]{2,1,0:T(8,128)S(1)} collective-permute-done((f32[4,32,128]{2,1,0:T(8,128)S(1)}, f32[4,32,128]{2,1,0:T(8,128)S(1)}, u32[]{:S(2)}, u32[]{:S(2)}) %collective-permute-start.4) | collective-permute-done | bytes 65568 | tf_op jit(solution)/shard_map/ppermute | solution.py:191
  41.7 0.0 collective-permute-done.5.rest_5_
  41.7 0.0 collective-permute-done.6.rest_6_
  41.8 13.9 %all_to_all.16 = f32[16,32,128]{2,1,0:T(8,128)S(1)} all-to-all(f32[16,32,128]{2,1,0:T(8,128)S(1)} %back.1), channel_id=1, replica_groups={{0,8,16,24,128,136,144,152,256,264,272,280,384,392,400,408},{32,40,48,5..., dimensions={0} | all-to-all | bytes 524288 | tf_op jit(solution)/shard_map/all_to_all | solution.py:201
  55.7 0.0 copy-start.3
  55.7 1.0 %mixed.1 = (f32[1024,512]{1,0:T(8,128)S(1)}, f32[8,8,128]{2,1,0:T(8,128)S(1)}) custom-call(bf16[1024,512]{1,0:T(8,128)(2,1)S(1)} %copy-done.2, bf16[640,512]{1,0:T(8,128)(2,1)S(1)} %get-tuple-element.27.top_queries, f32[1024,512]{1,0:T(8,128)S(1)} %get-tuple-element.28.local, f32[4,128,128]{2,1,0:T(8,128)S(1)} %bitcast.3, ...), custom_call_target="tpu_custom_call" | custom-call | flops 134217728 | bytes 5242880 | tf_op jit(solution)/shard_map/mixed/pallas_call | solution.py:281
  56.7 9.7 %all_to_all.17.squares = f32[8,8,128]{2,1,0:T(8,128)S(1)} all-to-all(f32[8,8,128]{2,1,0:T(8,128)S(1)} %get-tuple-element.34), channel_id=1, replica_groups=mesh['ctx'=64,'tp'=8] {'tp'}, dimensions={0} | all-to-all | bytes 65536 | tf_op jit(solution)/shard_map/all_to_all | solution.py:332
  66.4 0.0 copy-done.3
  66.4 1.2 %scored.1 = bf16[1024,512]{1,0:T(8,128)(2,1)} custom-call(f32[1024,512]{1,0:T(8,128)S(1)} %get-tuple-element.33.mixed, f32[8,8,128]{2,1,0:T(8,128)S(1)} %all_to_all.17.squares, f32[1,512]{1,0:T(1,128)S(1)} %bitcast.5), custom_call_target="tpu_custom_call" | custom-call | tf_op jit(solution)/shard_map/scored/pallas_call | solution.py:317
  (4 shorter events, 0.1 us)
Async XLA Ops:
  0.0 34.2 %copy-start.1 = (bf16[1024,512]{1,0:T(8,128)(2,1)S(1)}, bf16[1024,512]{1,0:T(8,128)(2,1)}, u32[]{:S(2)}) copy-start(bf16[1024,512]{1,0:T(8,128)(2,1)} %values.5) | copy-start | bytes 3145732
  0.0 34.2 %copy-start = (bf16[1024,512]{1,0:T(8,128)(2,1)S(1)}, bf16[1024,512]{1,0:T(8,128)(2,1)}, u32[]{:S(2)}) copy-start(bf16[1024,512]{1,0:T(8,128)(2,1)} %keys.5) | copy-start | bytes 3145732
  0.0 34.2 %copy-start.2 = (bf16[1024,512]{1,0:T(8,128)(2,1)S(1)}, bf16[1024,512]{1,0:T(8,128)(2,1)}, u32[]{:S(2)}) copy-start(bf16[1024,512]{1,0:T(8,128)(2,1)} %queries.5) | copy-start | bytes 3145732
  21.4 12.9 %collective-permute-start = (f32[3,32,128]{2,1,0:T(8,128)S(1)}, f32[3,32,128]{2,1,0:T(8,128)S(1)}, u32[]{:S(2)}, u32[]{:S(2)}) collective-permute-start(f32[3,32,128]{2,1,0:T(8,128)S(1)} %get-tuple-element.21), channel_id=1, source_target_pairs={{64,32},{96,0},{72,40},{104,8},{80,48},{112,16},{88,56},{120,24},{... | collective-permute-start | bytes 147464 | tf_op jit(solution)/shard_map/ppermute | solution.py:191
  22.7 13.4 %collective-permute-start.1 = (f32[3,32,128]{2,1,0:T(8,128)S(1)}, f32[3,32,128]{2,1,0:T(8,128)S(1)}, u32[]{:S(2)}, u32[]{:S(2)}) collective-permute-start(f32[3,32,128]{2,1,0:T(8,128)S(1)} %get-tuple-element.22.rest_0_), channel_id=1, source_target_pairs={{64,0},{72,8},{80,16},{88,24},{192,128},{200,136},{208,144},{216,1... | collective-permute-start | bytes 147464 | tf_op jit(solution)/shard_map/ppermute | solution.py:191
  23.4 12.8 %collective-permute-start.2 = (f32[4,32,128]{2,1,0:T(8,128)S(1)}, f32[4,32,128]{2,1,0:T(8,128)S(1)}, u32[]{:S(2)}, u32[]{:S(2)}) collective-permute-start(f32[4,32,128]{2,1,0:T(8,128)S(1)} %get-tuple-element.23), channel_id=1, source_target_pairs={{0,96},{32,0},{8,104},{40,8},{16,112},{48,16},{24,120},{56,24},{12... | collective-permute-start | bytes 196616 | tf_op jit(solution)/shard_map/ppermute | solution.py:191
  24.7 14.7 %collective-permute-start.3 = (f32[4,32,128]{2,1,0:T(8,128)S(1)}, f32[4,32,128]{2,1,0:T(8,128)S(1)}, u32[]{:S(2)}, u32[]{:S(2)}) collective-permute-start(f32[4,32,128]{2,1,0:T(8,128)S(1)} %get-tuple-element.30), channel_id=1, source_target_pairs={{0,32},{64,96},{8,40},{72,104},{16,48},{80,112},{24,56},{88,120},{... | collective-permute-start | bytes 196616 | tf_op jit(solution)/shard_map/ppermute | solution.py:191
  26.0 15.7 %collective-permute-start.4 = (f32[4,32,128]{2,1,0:T(8,128)S(1)}, f32[4,32,128]{2,1,0:T(8,128)S(1)}, u32[]{:S(2)}, u32[]{:S(2)}) collective-permute-start(f32[4,32,128]{2,1,0:T(8,128)S(1)} %get-tuple-element.31), channel_id=1, source_target_pairs={{32,96},{96,32},{40,104},{104,40},{48,112},{112,48},{56,120},{120,... | collective-permute-start | bytes 196616 | tf_op jit(solution)/shard_map/ppermute | solution.py:191
  34.3 7.4 %collective-permute-start.5 = (f32[4,32,128]{2,1,0:T(8,128)S(1)}, f32[4,32,128]{2,1,0:T(8,128)S(1)}, u32[]{:S(2)}, u32[]{:S(2)}) collective-permute-start(f32[4,32,128]{2,1,0:T(8,128)S(1)} %get-tuple-element.32), channel_id=1, source_target_pairs={{32,64},{40,72},{48,80},{56,88},{160,192},{168,200},{176,208},{184... | collective-permute-start | bytes 196616 | tf_op jit(solution)/shard_map/ppermute | solution.py:191
  36.1 5.5 %collective-permute-start.6 = (f32[4,32,128]{2,1,0:T(8,128)S(1)}, f32[4,32,128]{2,1,0:T(8,128)S(1)}, u32[]{:S(2)}, u32[]{:S(2)}) collective-permute-start(f32[4,32,128]{2,1,0:T(8,128)S(1)} %relay.1.rest_0_), channel_id=1, source_target_pairs={{96,64},{104,72},{112,80},{120,88},{224,192},{232,200},{240,208},{... | collective-permute-start | bytes 196616 | tf_op jit(solution)/shard_map/ppermute | solution.py:191
  55.7 10.7 %copy-start.3 = (f32[512]{0:T(512)S(1)}, f32[512]{0:T(512)}, u32[]{:S(2)}) copy-start(f32[512]{0:T(512)} %param.7) | copy-start | bytes 6148
